TPU v7x, 32 devices: a whole 2x2x4 slice. The times are simulated.
32 devices in a mesh: frames: 16 (over z, x, core), heads: 2 (over y).
Axes of the slice: x: 2, y: 2, z: 4, core: 2. Of those that a mesh axis runs over, the one named last changes fastest.
Arguments:
- query_states: bfloat16 [24576, 1024], P('frames', 'heads'), may hold values from -9 to 9
- key_states: bfloat16 [24576, 1024], P('frames', 'heads'), may hold values from -9 to 9
- value_states: bfloat16 [24576, 1024], P('frames', 'heads'), may hold values from -6 to 6
- pair_list: int32 [1024, 2], replicated, may hold values from 0 to 127, as said below
- out_weight: bfloat16 [1024, 1024], P('heads'), may hold values from -0.1875 to 0.1875
Outputs:
- attended: bfloat16 [24576, 1024], P('frames', 'heads')
Inputs may be any that keep to these rules, and one draw needn't show every extreme that they name: `pair_list`: row r belongs to device r // 64 of frames: its first frame is held by that device (frames f * 8 to f * 8 + 7 on device f), its second frame j lies on device j // 8. Among the 64 rows of one device at most 4 have their second frame on any one device, and some device is reached exactly 4 times. The two frames of a row differ.
All inputs are finite; a program needn't handle non-finite values.
Results may differ from a plain program's by a relative error of at most 0.017.
Values may be sent and summed in bfloat16 or wider, within the bound.
No kernel may reach another device: no remote copies, remote signals or barrier semaphores. Data moves between devices by JAX's collectives and lax.ppermute only.
A program may use at most 192 MiB of HBM per device.

v0:
```python
import math

import jax
import jax.numpy as jnp
from jax import lax
from jax.sharding import PartitionSpec as P

HDIM = 64
TOKF = 192


def attend(query_rows, key_rows, value_rows):
    number, length, columns = query_rows.shape
    heads_here = columns // HDIM
    queries = query_rows.reshape(number, length, heads_here, HDIM)
    keyed = key_rows.reshape(number, length, heads_here, HDIM)
    valued = value_rows.reshape(number, length, heads_here, HDIM)
    scores = jnp.einsum("bqhd,bkhd->bhqk", queries, keyed, preferred_element_type=jnp.float32) * (
        1.0 / math.sqrt(HDIM)
    )
    highest = jnp.max(scores, axis=-1, keepdims=True)
    exponent = jnp.exp(scores - highest)
    totals = jnp.sum(exponent, axis=-1, keepdims=True)
    weights = (exponent / totals).astype(jnp.bfloat16)
    output = jnp.einsum(
        "bhqk,bkhd->bqhd", weights, valued, preferred_element_type=jnp.float32
    ).astype(jnp.bfloat16)
    return (output.reshape(number, length, columns), (highest + jnp.log(totals))[..., 0])


def in_groups(arrays):
    number = arrays[0].shape[0]
    group_size = 1
    for candidate in range(1, number + 1):
        if number % candidate == 0 and candidate * arrays[0].shape[1] <= 1024:
            group_size = candidate
    stacked = tuple(
        (
            member_rows.reshape((number // group_size, group_size) + member_rows.shape[1:])
            for member_rows in arrays
        )
    )
    outputs, log_sums = lax.map(lambda grouped: attend(grouped[0], grouped[1], grouped[2]), stacked)
    return (
        outputs.reshape((number,) + outputs.shape[2:]),
        log_sums.reshape((number,) + log_sums.shape[2:]),
    )


def pick_rows(frames, frame_index, live_rows):
    picked = jnp.take(frames, frame_index, axis=0)
    return jnp.where(live_rows[:, None, None], picked, jnp.zeros_like(picked))


def slot_tables(pair_list, peer_count, frames_here, my_index):
    pair_rows = pair_list.shape[0] // peer_count
    capacity = (pair_rows + peer_count - 1) // peer_count
    first_frame = pair_list[:, 0].reshape(peer_count, pair_rows)
    second = pair_list[:, 1].reshape(peer_count, pair_rows)
    target = second // frames_here
    positions = jnp.arange(pair_rows)
    earlier = (target[:, :, None] == target[:, None, :]) & (
        positions[None, None, :] < positions[None, :, None]
    )
    peer_rank = jnp.sum(earlier.astype(jnp.int32), axis=2)
    slot_of_pair = target * capacity + peer_rank
    slot_ids = jnp.arange(peer_count * capacity)
    my_place = lax.dynamic_index_in_dim(slot_of_pair, my_index, 0, keepdims=False)
    my_first = (
        lax.dynamic_index_in_dim(first_frame, my_index, 0, keepdims=False) - my_index * frames_here
    )
    slot_hit = my_place[None, :] == slot_ids[:, None]
    own_live = jnp.any(slot_hit, axis=1)
    own_frame = jnp.sum(jnp.where(slot_hit, my_first[None, :], 0), axis=1)
    peer_match = (target == my_index)[:, None, :] & (
        peer_rank[:, None, :] == jnp.arange(capacity)[None, :, None]
    )
    peer_live = jnp.any(peer_match, axis=2).reshape(-1)
    local_second = second - my_index * frames_here
    peer_frame = jnp.sum(jnp.where(peer_match, local_second[:, None, :], 0), axis=2).reshape(-1)
    return (capacity, own_frame, own_live, peer_frame, peer_live)


def combine(sources, frames_here):
    outputs = jnp.concatenate([source[0] for source in sources], axis=0)
    log_sums = jnp.concatenate([source[1] for source in sources], axis=0)
    frame_ids = jnp.concatenate([source[2] for source in sources], axis=0)
    live_rows = jnp.concatenate([source[3] for source in sources], axis=0)
    number, length, columns = outputs.shape
    heads_here = columns // HDIM
    member = (frame_ids[:, None] == jnp.arange(frames_here)[None, :]) & live_rows[:, None]
    masked = jnp.where(member[:, :, None, None], log_sums[:, None], -jnp.inf)
    highest = jnp.max(masked, axis=0)
    reached = jnp.sum(jnp.where(member[:, :, None, None], highest[None], 0.0), axis=1)
    weight = jnp.exp(jnp.where(live_rows[:, None, None], log_sums - reached, -jnp.inf))
    member_float = member.astype(jnp.float32)
    totals = jnp.einsum("xf,xht->fht", member_float, weight, precision=lax.Precision.HIGHEST)
    weighted = (
        outputs.astype(jnp.float32).reshape(number, length, heads_here, HDIM)
        * jnp.transpose(weight, (0, 2, 1))[..., None]
    )
    summed = jnp.einsum("xf,xthd->fthd", member_float, weighted, precision=lax.Precision.HIGHEST)
    merged = summed / jnp.transpose(totals, (0, 2, 1))[..., None]
    return merged.reshape(frames_here * length, columns).astype(jnp.bfloat16)


def body(query_states, key_states, value_states, pair_list, out_weight):
    peer_count = lax.axis_size("frames")
    my_index = lax.axis_index("frames")
    columns = query_states.shape[1]
    frames_here = query_states.shape[0] // TOKF
    frame_query = query_states.reshape(frames_here, TOKF, columns)
    frame_key = key_states.reshape(frames_here, TOKF, columns)
    frame_value = value_states.reshape(frames_here, TOKF, columns)
    capacity, own_frame, own_live, peer_frame, peer_live = slot_tables(
        pair_list, peer_count, frames_here, my_index
    )
    slot_count = peer_count * capacity

    def to_peers(stacked):
        return stacked.reshape((peer_count, capacity) + stacked.shape[1:])

    def from_peers(stacked):
        return stacked.reshape((slot_count,) + stacked.shape[2:])

    self_out, self_lse = in_groups((frame_query, frame_key, frame_value))
    self_ids = jnp.arange(frames_here, dtype=jnp.int32)
    self_live = jnp.ones((frames_here,), dtype=bool)
    near_query = pick_rows(frame_query, own_frame, own_live)
    arrived = (
        lax.all_to_all(
            to_peers(pick_rows(frame_query, peer_frame, peer_live)),
            "frames",
            split_axis=0,
            concat_axis=0,
            tiled=True,
        ),
        lax.all_to_all(
            to_peers(pick_rows(frame_key, peer_frame, peer_live)),
            "frames",
            split_axis=0,
            concat_axis=0,
            tiled=True,
        ),
        lax.all_to_all(
            to_peers(pick_rows(frame_value, peer_frame, peer_live)),
            "frames",
            split_axis=0,
            concat_axis=0,
            tiled=True,
        ),
    )
    far_query, far_key, far_value = (from_peers(member_rows) for member_rows in arrived)
    ahead_out, ahead_lse = in_groups((near_query, far_key, far_value))
    back_out, back_lse = in_groups(
        (
            far_query,
            pick_rows(frame_key, own_frame, own_live),
            pick_rows(frame_value, own_frame, own_live),
        )
    )
    behind_out = from_peers(
        lax.all_to_all(to_peers(back_out), "frames", split_axis=0, concat_axis=0, tiled=True)
    )
    behind_lse = from_peers(
        lax.all_to_all(to_peers(back_lse), "frames", split_axis=0, concat_axis=0, tiled=True)
    )
    merged = combine(
        (
            (self_out, self_lse, self_ids, self_live),
            (ahead_out, ahead_lse, own_frame, own_live),
            (behind_out, behind_lse, peer_frame, peer_live),
        ),
        frames_here,
    )
    head_term = jnp.dot(merged, out_weight, preferred_element_type=jnp.float32)
    return lax.psum_scatter(
        head_term.astype(jnp.bfloat16), "heads", scatter_dimension=1, tiled=True
    )


def solution(mesh):
    placed = (
        P("frames", "heads"),
        P("frames", "heads"),
        P("frames", "heads"),
        P(),
        P("heads", None),
    )
    return jax.shard_map(
        body, mesh=mesh, in_specs=placed, out_specs=P("frames", "heads"), check_vma=False
    )
```

profile of v0, /device:TPU:0, one launch (start us, length us, event | category | flops | bytes accessed | tf_op | source)
XLA Modules:
  0.0 1424.7 jit_solution(5106480100870846387)
XLA Ops:
  9.0 8.5 gather_fusion.2
  17.5 8.7 gather_fusion.4
  26.2 7.2 gather_fusion
  33.5 21.0 %select_select_fusion.3 = (bf16[64,192,512]{2,1,0:T(8,128)(2,1)}, bf16[64,192,512]{2,1,0:T(8,128)(2,1)S(1)}, bf16[64,192,512]{2,1,0:T(8,128)(2,1)}) fusion(bf16[64,192,512]{2,1,0:T(8,128)(2,1)} %gather_fusion.2, pred[64]{0:T(512)(128)(4,1)S(1)} %get-tuple-element.244, pred[64]{0:T(512)(128)(4,1)S(1)} %reshape.300, bf16[64,192,512]{2,1,0:T(8,128)(2,1)} %gather_fusion.4, ...), kind=kLoop, calls=%fused_computation.48 | loop fusion | flops 37748736 | bytes 75497600 | tf_op jit(solution)/shard_map/jit(_where)/select_n | solution.py:52
  54.4 279.4 %all_to_all.25 = bf16[16,4,192,512]{3,2,1,0:T(8,128)(2,1)} all-to-all(bf16[16,4,192,512]{3,2,1,0:T(8,128)(2,1)S(1)} %bitcast.138), channel_id=1, replica_groups=mesh['frames'=16,'heads'=2] {'frames'}, dimensions={0} | all-to-all | bytes 25165824 | tf_op jit(solution)/shard_map/all_to_all | solution.py:131
  333.9 6.2 all-to-all-start
  340.0 8.7 gather_fusion.1
  348.8 7.2 gather_fusion.3
  356.0 8.7 gather_fusion.5
  364.8 24.5 %select_select_fusion.4 = (bf16[64,192,512]{2,1,0:T(8,128)(2,1)}, bf16[64,192,512]{2,1,0:T(8,128)(2,1)}, bf16[64,192,512]{2,1,0:T(8,128)(2,1)}) fusion(bf16[64,192,512]{2,1,0:T(8,128)(2,1)} %gather_fusion.1, pred[64]{0:T(512)(128)(4,1)S(1)} %get-tuple-element.243, pred[64]{0:T(512)(128)(4,1)S(1)} %fusion.17, bf16[64,192,512]{2,1,0:T(8,128)(2,1)} %gather_fusion.3, ...), kind=kLoop, calls=%fused_computation.49 | loop fusion | flops 37748736 | bytes 75497600 | tf_op jit(solution)/shard_map/jit(_where)/select_n | solution.py:52
  389.2 174.6 %all-to-all-done = bf16[16,4,192,512]{3,2,1,0:T(8,128)(2,1)} async-done(((bf16[16,4,192,512]{3,2,1,0:T(8,128)(2,1)}), bf16[16,4,192,512]{3,2,1,0:T(8,128)(2,1)}, u32[]{:S(2)}, u32[]{:S(2)}) %all-to-all-start) | async-done | bytes 12582944 | tf_op jit(solution)/shard_map/all_to_all | solution.py:145
  563.8 53.7 %all-to-all-start.1 = ((bf16[16,4,192,512]{3,2,1,0:T(8,128)(2,1)}), bf16[16,4,192,512]{3,2,1,0:T(8,128)(2,1)}, u32[]{:S(2)}, u32[]{:S(2)}) async-start(bf16[16,4,192,512]{3,2,1,0:T(8,128)(2,1)} %bitcast.136), calls=%async_computation.1 | async-start | bytes 25165824 | tf_op jit(solution)/shard_map/all_to_all | solution.py:138
  618.3 285.3 %while.38 = (s32[]{:T(128)}, bf16[16,4,192,512]{3,2,1,0:T(8,128)(2,1)}, f32[16,4,8,192]{3,2,1,0:T(8,128)}, bf16[16,4,192,512]{3,2,1,0:T(8,128)(2,1)}, bf16[16,4,...) while((s32[]{:T(128)}, bf16[16,4,192,512]{3,2,1,0:T(8,128)(2,1)}, ...), condition=%wide.region_16.18_spmd, body=%wide.region_13.17_spmd.sunk | while | flops 312993792 | bytes 33235072 | solution.py:43
  626.7 2.7 multiply_reduce_fusion.8
  630.6 2.5 fusion.72
  644.5 2.7 multiply_reduce_fusion.8
  662.4 2.7 multiply_reduce_fusion.8
  680.2 2.7 multiply_reduce_fusion.8
  698.0 2.7 multiply_reduce_fusion.8
  702.0 2.5 fusion.72
  715.8 2.7 multiply_reduce_fusion.8
  733.7 2.7 multiply_reduce_fusion.8
  737.7 2.5 fusion.72
  751.5 2.7 multiply_reduce_fusion.8
  755.5 2.5 fusion.72
  769.4 2.7 multiply_reduce_fusion.8
  773.4 2.5 fusion.72
  787.2 2.7 multiply_reduce_fusion.8
  805.0 2.7 multiply_reduce_fusion.8
  822.8 2.7 multiply_reduce_fusion.8
  840.7 2.7 multiply_reduce_fusion.8
  858.5 2.7 multiply_reduce_fusion.8
  862.5 2.5 fusion.72
  876.3 2.7 multiply_reduce_fusion.8
  894.2 2.7 multiply_reduce_fusion.8
  903.6 6.2 all-to-all-start.4
  909.8 28.6 %while.36 = (s32[]{:T(128)}, bf16[2,4,192,512]{2,3,1,0:T(8,128)(2,1)}, f32[2,4,8,192]{3,2,1,0:T(8,128)S(1)}, bf16[2,4,192,512]{3,2,1,0:T(8,128)(2,1)S(1)}, bf16[...) while((s32[]{:T(128)}, bf16[2,4,192,512]{2,3,1,0:T(8,128)(2,1)}, ...), condition=%wide.region_8.9_spmd, body=%wide.region_5.8_spmd.sunk | while | flops 312993792 | bytes 44785848 | solution.py:43
  917.2 2.7 multiply_reduce_fusion.6
  931.4 2.7 multiply_reduce_fusion.6
  938.7 6.0 all-to-all-start.3
  945.7 197.7 %while.37 = (s32[]{:T(128)}, bf16[16,4,192,512]{2,3,1,0:T(8,128)(2,1)}, f32[16,4,8,192]{3,2,1,0:T(8,128)}, bf16[16,4,192,512]{3,2,1,0:T(8,128)(2,1)}, bf16[16,4,...) while((s32[]{:T(128)}, bf16[16,4,192,512]{2,3,1,0:T(8,128)(2,1)}, ...), condition=%wide.region_12.14_spmd, body=%wide.region_9.13_spmd.sunk | while | flops 312993792 | bytes 31924352 | solution.py:43
  1150.4 18.1 %all-to-all-done.3 = bf16[16,4,192,512]{3,2,1,0:T(8,128)(2,1)} async-done(((bf16[16,4,192,512]{3,2,1,0:T(8,128)(2,1)}), bf16[16,4,192,512]{3,2,1,0:T(8,128)(2,1)}, u32[]{:S(2)}, u32[]{:S(2)}) %all-to-all-start.3) | async-done | bytes 12582944 | tf_op jit(solution)/shard_map/all_to_all | solution.py:163
  1168.5 20.7 %copy.94 = bf16[16,4,192,512]{2,3,1,0:T(8,128)(2,1)} copy(bf16[16,4,192,512]{3,2,1,0:T(8,128)(2,1)} %all-to-all-done.3) | data formatting | bytes 25165824 | tf_op jit(solution)/shard_map/all_to_all | solution.py:163
  1189.2 34.9 %convert_multiply_fusion = f32[136,192,8,64]{1,3,2,0:T(8,128)} fusion(bf16[64,192,8,64]{1,3,2,0:T(8,128)(2,1)} %bitcast.135, bf16[64,192,8,64]{1,3,2,0:T(8,128)(2,1)} %bitcast.148, bf16[8,192,8,64]{1,3,2,0:T(8,128)(2,1)} %bitcast.152, f32[136,192,8]{1,2,0:T(8,128)S(1)} %bitcast.149), kind=kLoop, calls=%fused_computation.44 | loop fusion | flops 53477376 | bytes 81051648 | tf_op jit(solution)/shard_map/mul | solution.py:99
  1224.1 93.7 %divide_convert_fusion.12 = bf16[8,192,8,64]{1,0,3,2:T(8,128)(2,1)S(1)} fusion(f32[136,192,8,64]{1,3,2,0:T(8,128)} %convert_multiply_fusion, f32[8,192,8]{1,0,2:T(8,128)S(1)} %convolution_bitcast_fusion, s32[136]{0:T(256)S(1)} %pad_add_fusion.1, pred[136]{0:T(512)(128)(4,1)S(1)} %pad_add_fusion), kind=kOutput, calls=%fused_computation.53 | convolution fusion | flops 1285032064 | bytes 55100072 | tf_op jit(solution)/shard_map/xf,xthd->fthd/dot_general | solution.py:102
  1317.8 2.8 convert_element_type.47
  1320.5 4.9 convolution_convert_fusion
  1325.4 92.2 %reduce-scatter.2.cloned.1.call-done = bf16[1536,512]{1,0:T(8,128)(2,1)} async-done(((bf16[1536,1024]{1,0:T(8,128)(2,1)}), bf16[1536,512]{1,0:T(8,128)(2,1)}) %reduce-scatter.2.cloned.1.call-update) | async-done | bytes 1572880 | tf_op jit(solution)/shard_map/reduce_scatter | solution.py:177
  (470 shorter events, 458.7 us)
Async XLA Ops:
  6.5 1314.0 %copy-start = (bf16[512,1024]{1,0:T(8,128)(2,1)S(1)}, bf16[512,1024]{1,0:T(8,128)(2,1)}, u32[]{:S(2)}) copy-start(bf16[512,1024]{1,0:T(8,128)(2,1)} %param.17) | copy-start | bytes 3145732
  8.4 9.1 copy-start.7
  8.6 8.9 copy-start.11
  9.0 24.5 %copy-start.9 = (pred[64]{0:T(512)(128)(4,1)}, pred[64]{0:T(512)(128)(4,1)S(1)}, u32[]{:S(2)}) copy-start(pred[64]{0:T(512)(128)(4,1)S(1)} %reshape.300) | copy-start | bytes 196
  17.5 8.7 copy-start.1
  333.9 229.9 %all-to-all-start = ((bf16[16,4,192,512]{3,2,1,0:T(8,128)(2,1)}), bf16[16,4,192,512]{3,2,1,0:T(8,128)(2,1)}, u32[]{:S(2)}, u32[]{:S(2)}) async-start(bf16[16,4,192,512]{3,2,1,0:T(8,128)(2,1)} %bitcast.137), calls=%async_computation | async-start | bytes 25165824 | tf_op jit(solution)/shard_map/all_to_all | solution.py:145
  364.7 24.5 %copy-start.13 = (pred[64]{0:T(512)(128)(4,1)}, pred[64]{0:T(512)(128)(4,1)S(1)}, u32[]{:S(2)}) copy-start(pred[64]{0:T(512)(128)(4,1)S(1)} %fusion.17) | copy-start | bytes 196
  563.8 339.9 %all-to-all-start.1 = ((bf16[16,4,192,512]{3,2,1,0:T(8,128)(2,1)}), bf16[16,4,192,512]{3,2,1,0:T(8,128)(2,1)}, u32[]{:S(2)}, u32[]{:S(2)}) async-start(bf16[16,4,192,512]{3,2,1,0:T(8,128)(2,1)} %bitcast.136), calls=%async_computation.1 | async-start | bytes 25165824 | tf_op jit(solution)/shard_map/all_to_all | solution.py:138
  626.7 3.9 copy-start.2
  644.5 3.9 copy-start.2
  662.4 3.9 copy-start.2
  680.2 3.9 copy-start.2
  698.0 4.0 copy-start.2
  715.8 3.9 copy-start.2
  733.7 3.9 copy-start.2
  751.5 3.9 copy-start.2
  769.4 3.9 copy-start.2
  787.2 3.9 copy-start.2
  805.0 3.9 copy-start.2
  822.8 3.9 copy-start.2
  840.6 3.9 copy-start.2
  858.5 4.0 copy-start.2
  876.3 3.9 copy-start.2
  894.2 3.9 copy-start.2
  903.6 35.1 %all-to-all-start.4 = ((f32[16,4,8,192]{3,2,1,0:T(8,128)}), f32[16,4,8,192]{3,2,1,0:T(8,128)}, u32[]{:S(2)}, u32[]{:S(2)}) async-start(f32[16,4,8,192]{3,2,1,0:T(8,128)} %get-tuple-element.110), calls=%async_computation.4 | async-start | bytes 1048576 | tf_op jit(solution)/shard_map/all_to_all | solution.py:166
  909.8 28.6 %copy-start.10 = (pred[64]{0:T(512)(128)(4,1)S(1)}, pred[64]{0:T(512)(128)(4,1)}, u32[]{:S(2)}) copy-start(pred[64]{0:T(512)(128)(4,1)} %copy-done.9) | copy-start | bytes 196
  909.8 28.6 %copy-start.14 = (pred[64]{0:T(512)(128)(4,1)S(1)}, pred[64]{0:T(512)(128)(4,1)}, u32[]{:S(2)}) copy-start(pred[64]{0:T(512)(128)(4,1)} %copy-done.13) | copy-start | bytes 196
  909.8 28.7 %copy-start.8 = (s32[64]{0:T(128)S(1)}, s32[64]{0:T(128)}, u32[]{:S(2)}) copy-start(s32[64]{0:T(128)} %copy-done.7) | copy-start | bytes 772
  909.8 28.7 %copy-start.12 = (s32[64]{0:T(128)S(1)}, s32[64]{0:T(128)}, u32[]{:S(2)}) copy-start(s32[64]{0:T(128)} %copy-done.11) | copy-start | bytes 772
  917.2 3.9 copy-start.3
  931.4 4.0 copy-start.3
  938.7 229.8 %all-to-all-start.3 = ((bf16[16,4,192,512]{3,2,1,0:T(8,128)(2,1)}), bf16[16,4,192,512]{3,2,1,0:T(8,128)(2,1)}, u32[]{:S(2)}, u32[]{:S(2)}) async-start(bf16[16,4,192,512]{3,2,1,0:T(8,128)(2,1)} %get-tuple-element.107), calls=%async_computation.3 | async-start | bytes 25165824 | tf_op jit(solution)/shard_map/all_to_all | solution.py:163
  944.7 472.9 %reduce-scatter.2.cloned.1.call-start = ((), (), s32[]{:S(2)}) async-start(), calls=%async_computation.6 | async-start | bytes 4718592 | tf_op jit(solution)/shard_map/reduce_scatter | solution.py:177
  952.5 2.3 copy-start.4
  977.3 2.3 copy-start.4
  989.6 2.3 copy-start.4
  1001.9 2.3 copy-start.4
  1014.4 2.3 copy-start.4
  1026.7 2.3 copy-start.4
  1039.0 2.3 copy-start.4
  1051.4 2.3 copy-start.4
  1063.8 2.3 copy-start.4
  1076.1 2.3 copy-start.4
  1088.5 2.3 copy-start.4
  1100.8 2.3 copy-start.4
  1113.1 2.3 copy-start.4
  1125.5 2.3 copy-start.4
  1137.8 2.3 copy-start.4
  (5 other events, 8.1 us)
Sparse Core Ops, SparseCore 0:
  1325.6 92.0 reduce-scatter.1
where the time goes:
time: 1440 us; the launch traced here: 1420 us
  local copies, waits for them, and re-layouts  393 us (27%)
  waiting for transfers between devices  285 us (20%)
  blocking collectives  279 us (19%)
  matrix products  230 us (16%)
  other arithmetic  150 us (10%)
  starting transfers between devices  72 us (5%)
    all_to_all x1, blocking collectives, body(): lax.all_to_all(to_peers(pick_rows(frame_query, peer_frame, peer_live)), '...  279 us
    dynamic_slice x170, local copies, waits for them, and re-layouts, in_groups(): lax.map(lambda grouped: attend(grouped[0], grouped[1], grouped[2]), stacked)  258 us
    all_to_all x1, waiting for transfers between devices, body(): lax.all_to_all(to_peers(pick_rows(frame_value, peer_frame, peer_live)), '...  175 us
    dot_general x1, matrix products, combine(): jnp.einsum('xf,xthd->fthd', member_float, weighted, precision=lax.Precisi...  93.7 us
    reduce_scatter x1, waiting for transfers between devices, body(): lax.psum_scatter(head_term.astype(jnp.bfloat16), 'heads', scatter_dimensi...  92.2 us
    dot_general x34, matrix products, attend(): jnp.einsum('bhqk,bkhd->bqhd', weights, valued, preferred_element_type=jnp...  66 us
    dot_general x34, matrix products, attend(): jnp.einsum('bqhd,bkhd->bhqk', queries, keyed, preferred_element_type=jnp....  65 us
    dynamic_update_slice x50, local copies, waits for them, and re-layouts, in_groups(): lax.map(lambda grouped: attend(grouped[0], grouped[1], grouped[2]), stacked)  55.8 us
  transfers between devices with their start and end apart: 5, of which 3 were waited for; matrix products, arithmetic and copies ran while one was open for 40% of the time, Pallas kernels for 0%

commit v1 on v0

v1 whole, which is shorter than its diff:
```python
import functools

import jax
import jax.numpy as jnp
from jax import lax
from jax.experimental import pallas as pl
from jax.experimental.pallas import tpu as pltpu
from jax.sharding import PartitionSpec as P

HDIM = 64
TOKF = 192
LANES = 128
PACKED = 2 * TOKF
GROUP = 4
SHIFT = 16
DEAD = 1 << 30
UNROLL = 2
LOW, HIGH = 2.0**-60, 2.0**100
NEVER = -1e30
VMEM_LIMIT = 60 * 1024 * 1024


def table_kernel(planes, plane_size, group, frames_here, place_ref, ends_ref, table_ref):
    block = pl.program_id(0)
    plane, place = place_ref[0], place_ref[1]
    assert planes in (1, 4)
    plane_frames = plane_size * frames_here
    key_frames = group * frames_here
    query_frames = planes * frames_here
    width = table_ref.shape[2]
    tiles = ends_ref.shape[1]
    step = 2 * UNROLL

    def bits(size):
        assert size & (size - 1) == 0
        return size.bit_length() - 1

    def iota(shape, axis):
        return lax.broadcasted_iota(jnp.int32, shape, axis)

    candidates = []
    for side in range(2):
        for tile in range(tiles):
            pair = [ends_ref[end, tile : tile + 1] ^ (plane << bits(plane_frames)) for end in (side, 1 - side)]
            candidates.append((pair[0], pair[1], None))
    lane = iota((1, LANES), 1)
    chunk = lane >> bits(frames_here)
    mine = (
        ((((chunk & 1) << 1) + (((chunk >> 1) ^ chunk) & 1)) << bits(plane_frames))
        + (place << bits(frames_here))
        + (lane & (frames_here - 1))
    )
    candidates.append((mine, mine, lane < query_frames))

    lives, queries, keys, hits = [], [], [], []
    for asked, key, valid in candidates:
        live = (key >> bits(key_frames) == block) & (
            (asked >> bits(frames_here)) & (plane_size - 1) == place
        )
        if valid is not None:
            live = live & valid
        distance = asked >> bits(plane_frames)
        chunk = ((distance ^ (distance >> 1)) & 1) * 2 + (distance >> 1)
        query = (chunk << bits(frames_here)) + (asked & (frames_here - 1))
        query = jnp.where(live, query, query_frames)
        lives.append(live)
        queries.append(query)
        keys.append(key & (key_frames - 1))
        hits.append(jnp.where(query == iota((query_frames, LANES), 0), 1.0, 0.0))
    stacked = jnp.concatenate(hits, axis=0).astype(jnp.bfloat16)

    def product(left, right):
        return jnp.dot(left.astype(jnp.bfloat16), right.astype(jnp.bfloat16), preferred_element_type=jnp.float32)

    def ones_where(condition):
        return jnp.where(condition, 1.0, 0.0)

    square = (LANES, LANES)
    earlier = product(stacked, ones_where(iota(square, 0) < iota(square, 1)))
    every = product(stacked, jnp.ones(square, jnp.float32))
    before = [jnp.zeros((query_frames, LANES), jnp.float32)]
    for tile in range(len(hits)):
        before.append(before[-1] + every[tile * query_frames : (tile + 1) * query_frames])
    used = 2.0 * jnp.floor((before[-1] + 1.0) * 0.5)
    square = (query_frames, query_frames)
    row, column = iota(square, 0), iota(square, 1)
    row_chunk, column_chunk = row >> bits(frames_here), column >> bits(frames_here)
    inside = product(ones_where((row_chunk == column_chunk) & (column < row)), used)
    whole = product(ones_where(row_chunk == column_chunk), used)
    steps = jnp.floor((whole + (step - 1.0)) * (1.0 / step))
    leads = column & (frames_here - 1) == 0
    chunk_start = product(ones_where((column_chunk < row_chunk) & leads), steps)
    start = inside + step * chunk_start

    frame = iota((query_frames, LANES), 0)
    at = iota((query_frames, LANES), 1)
    first = frame & (frames_here - 1) == 0
    starts = jnp.where(first & (at == frame >> bits(frames_here)), chunk_start, 0.0)
    starts = starts + jnp.where(first & (at == planes), steps, 0.0)
    starts = jnp.sum(starts, axis=0, keepdims=True).astype(jnp.int32)

    placed, values = [], []
    for tile, hit in enumerate(hits):
        rank = earlier[tile * query_frames : (tile + 1) * query_frames] + before[tile] + start
        slot = jnp.sum(hit * rank, axis=0, keepdims=True).astype(jnp.int32)
        slot = jnp.where(lives[tile], slot, -1)
        placed.append(ones_where(slot == iota((width, LANES), 0)).astype(jnp.bfloat16))
        kind = iota((8, LANES), 0)
        value = jnp.where(kind == 0, queries[tile], jnp.where(kind == 1, keys[tile], 1))
        values.append(value.astype(jnp.float32).astype(jnp.bfloat16))
    codes = lax.dot_general(
        jnp.concatenate(values, axis=1),
        jnp.concatenate(placed, axis=1),
        (((1,), (1,)), ((), ())),
        preferred_element_type=jnp.float32,
    ).astype(jnp.int32)
    code = jnp.where(codes[2:3] > 0, (codes[0:1] << SHIFT) + codes[1:2], DEAD)
    starts = jnp.concatenate([starts] * (width // LANES), axis=1)
    table_ref[0] = jnp.where(iota((2, width), 0) == 0, code, starts)


def attend_table(pair_list, planes, plane_size, group, frames_here, places):
    peers = planes * plane_size
    rows = pair_list.shape[0]
    blocks = peers // group
    number = 2 * planes * group * (rows // peers // peers) + frames_here
    most = number + planes * frames_here + planes * (2 * UNROLL - 2)
    width = (most + LANES - 1) // LANES * LANES
    ends = pair_list.T.reshape(2, rows // LANES, LANES)
    return pl.pallas_call(
        functools.partial(table_kernel, planes, plane_size, group, frames_here),
        grid=(blocks,),
        in_specs=[
            pl.BlockSpec(memory_space=pltpu.SMEM),
            pl.BlockSpec(ends.shape, lambda block: (0, 0, 0)),
        ],
        out_specs=pl.BlockSpec((1, 2, width), lambda block: (block, 0, 0)),
        out_shape=jax.ShapeDtypeStruct((blocks, 2, width), jnp.int32),
        compiler_params=pltpu.CompilerParams(vmem_limit_bytes=VMEM_LIMIT),
    )(places, ends)


def attend_kernel(
    begin, number, chunks, sources, states, ends, table_ref, place_ref, order_ref, *refs
):
    del order_ref
    query_refs, refs = refs[: len(chunks)], refs[len(chunks) :]
    pair_refs = []
    for parts in sources:
        pair_refs.append(refs[:parts])
        refs = refs[parts:]
    state_refs, refs = refs[: 2 * states], refs[2 * states :]
    done_ref, refs = refs[0], refs[1:]
    done_ref[...] = jnp.zeros_like(done_ref)
    outs = len(chunks) if ends else 2
    out_refs, refs = refs[:outs], refs[outs:]
    sum_ref, total_ref, pair_ref, wide_ref, query_ref, score_ref, arrived, left = refs[:8]
    frames_here = query_refs[0].shape[0]
    group = pair_ref.shape[1]
    per_source = max(pair_refs[0][0].shape[0] // group, 1)
    first_frame = chunks[0] * frames_here
    query_frames = len(chunks) * frames_here
    held_from = 0 if ends else begin

    def copies(block, slot, source):
        refs_here = pair_refs[source]
        if len(refs_here) == 1:
            part = refs_here[0].at[pl.ds(block % per_source * group, group)]
            return [pltpu.make_async_copy(part, pair_ref.at[slot], arrived.at[slot])]
        result = []
        for far, ref in enumerate(refs_here):
            here = pair_ref.at[slot, pl.ds((place_ref[1] // 2 ^ far) * 2, 2)]
            result.append(pltpu.make_async_copy(ref, here, arrived.at[slot]))
        return result

    def fetch(block, slot):
        for source in range(len(sources)):

            @pl.when((block - held_from) // per_source == source)
            def _():
                for copy in copies(block, slot, source):
                    copy.start()

    def over_blocks(first_block, turns, step, ahead=None, before=None, behind=None):
        def visit(turn, carry):
            block = first_block + turn

            @pl.when(turn + 1 < turns)
            def _():
                fetch(block + 1, (turn + 1) % 2)

            whole = pair_ref.at[turn % 2]
            pltpu.make_async_copy(whole, whole, arrived.at[turn % 2]).wait()

            def units_of(index):
                first = index * 2 * UNROLL
                codes = [table_ref[block, 0, first + member] for member in range(2 * UNROLL)]
                return [codes[2 * unit : 2 * unit + 2] for unit in range(UNROLL)]

            def several(index, inner):
                step(turn % 2, units_of(index), units_of(index + 1) if ahead else None)
                return inner

            for index, chunk in enumerate(chunks):
                if before:
                    before(index)
                begins = table_ref[block, 1, chunk]
                if ahead:
                    ahead(turn % 2, units_of(begins))
                lax.fori_loop(begins, table_ref[block, 1, chunk + 1], several, 0)
                if behind:
                    behind(index)
            return carry

        if turns == 1:
            visit(0, 0)
        else:
            lax.fori_loop(0, turns, visit, 0)

    def frames_at(slot, unit):
        keys = []
        for code in unit:
            key_frame = code & ((1 << SHIFT) - 1)
            keys.append((slot, key_frame // frames_here, key_frame % frames_here))
        here = (unit[0] >> SHIFT) - first_frame
        return jnp.where((here >= 0) & (here < query_frames), here, 0), keys

    def scores_of(slot, unit):
        query_frame, keys = frames_at(slot, unit)
        held = jnp.concatenate([pair_ref[slot, device, 0, frame] for slot, device, frame in keys], axis=0)
        return lax.dot_general(
            wide_ref[query_frame], held, (((1,), (1,)), ((), ())), preferred_element_type=jnp.float32
        )

    def bias_of(unit):
        lane = lax.broadcasted_iota(jnp.int32, (1, PACKED), 1)
        bias = [jnp.where(code < DEAD, 0.0, NEVER) for code in unit]
        return jnp.where(lane < TOKF, bias[0], bias[1])

    def sums_of(keys, weights):
        held = jnp.concatenate([pair_ref[slot, device, 1, frame] for slot, device, frame in keys], axis=0)
        return by_head(
            jnp.dot(weights.astype(jnp.bfloat16), held, preferred_element_type=jnp.float32)
        )

    def by_head(both):
        lane = lax.broadcasted_iota(jnp.int32, (TOKF, LANES), 1)
        return jnp.where(lane < HDIM, both[:TOKF], both[TOKF:])

    def totals_of(weights):
        folded = weights[:, :LANES] + weights[:, LANES : 2 * LANES] + weights[:, 2 * LANES :]
        return by_head(folded + pltpu.roll(folded, HDIM, 1))

    def look_ahead(slot, units):
        for place, unit in enumerate(units):
            score_ref[place] = scores_of(slot, unit)

    def plain(slot, units, following):
        results = []
        for place, unit in enumerate(units):
            query_frame, keys = frames_at(slot, unit)
            weights = jnp.exp(score_ref[place] + bias_of(unit))
            score_ref[place] = scores_of(slot, following[place])
            results.append((query_frame, sums_of(keys, weights), totals_of(weights)))
        for query_frame, summed, total in results:
            sum_ref[query_frame] += summed
            total_ref[query_frame] += total

    asked = [
        pltpu.make_async_copy(ref, query_ref.at[index], left.at[index])
        for index, ref in enumerate(query_refs)
    ]
    for copy in asked:
        copy.start()
    fetch(begin, 0)
    frames_of = [pl.ds(index * frames_here, frames_here) for index in range(len(chunks))]
    taken, put = [], []
    for piece in range(states):
        old_refs = state_refs[2 * piece : 2 * piece + 2]
        pieces_chunks = old_refs[0].shape[0] // frames_here
        for index in range(pieces_chunks):
            if len(taken) == len(chunks):
                break
            begin_chunk = chunks[0] if states == 1 and pieces_chunks > len(chunks) else 0
            source = pl.ds((begin_chunk + index) * frames_here, frames_here)
            place = len(taken)
            taken.append(
                [
                    pltpu.make_async_copy(
                        old_ref.at[source], new_ref.at[frames_of[place]], arrived.at[2 + place]
                    )
                    for old_ref, new_ref in zip(old_refs, (sum_ref, total_ref))
                ]
            )
    for copies_here in taken:
        for copy in copies_here:
            copy.start()

    def widen(index):
        asked[index].wait()

        def one(frame, carry):
            rows = query_ref[index, frame] * jnp.asarray(HDIM**-0.5, wide_ref.dtype)
            first = lax.broadcasted_iota(jnp.int32, rows.shape, 1) < HDIM
            zeros = jnp.zeros_like(rows)
            wide_ref[index * frames_here + frame, :TOKF] = jnp.where(first, rows, zeros)
            wide_ref[index * frames_here + frame, TOKF:] = jnp.where(first, zeros, rows)
            return carry

        lax.fori_loop(0, frames_here, one, 0, unroll=4)

    def clear(frame, carry):
        sum_ref[frame] = jnp.zeros(sum_ref.shape[1:], sum_ref.dtype)
        total_ref[frame] = jnp.zeros(total_ref.shape[1:], total_ref.dtype)
        return carry

    for index in range(len(chunks)):
        widen(index)
    if not states:
        lax.fori_loop(0, query_frames, clear, 0, unroll=4)

    def enter(index):
        if states:
            for ref in (sum_ref, total_ref):
                part = ref.at[frames_of[index]]
                pltpu.make_async_copy(part, part, arrived.at[2 + index]).wait()

    def leave(index):
        if not ends:
            for ref, out in zip((sum_ref, total_ref), out_refs):
                copy = pltpu.make_async_copy(
                    ref.at[frames_of[index]], out.at[frames_of[index]], left.at[index]
                )
                copy.start()
                put.append(copy)

    if number == 1:
        over_blocks(begin, number, plain, look_ahead, enter, leave)
    else:
        for index in range(len(chunks)):
            enter(index)
        over_blocks(begin, number, plain, look_ahead)
        for index in range(len(chunks)):
            leave(index)
    for copy in put:
        copy.wait()
    if not ends:
        return
    whole_ref, top_ref = refs[8:]

    def gather_totals(frame, carry):
        total = total_ref[frame]
        square = (LANES, LANES)
        same = lax.broadcasted_iota(jnp.int32, square, 0) // HDIM == lax.broadcasted_iota(jnp.int32, square, 1) // HDIM
        ones = jnp.where(same, 1.0, 0.0).astype(jnp.bfloat16)
        high = total.astype(jnp.bfloat16)
        low = (total - high.astype(jnp.float32)).astype(jnp.bfloat16)
        whole_ref[frame] = jnp.dot(high, ones, preferred_element_type=jnp.float32) + jnp.dot(
            low, ones, preferred_element_type=jnp.float32
        )
        return carry

    lax.fori_loop(0, query_frames, gather_totals, 0, unroll=4)
    within = (jnp.min(whole_ref[...]) > LOW) & (jnp.max(whole_ref[...]) < HIGH)

    @pl.when(jnp.logical_not(within))
    def _():
        lax.fori_loop(0, query_frames, clear, 0)
        top_ref[...] = jnp.full_like(top_ref, 2 * NEVER)

        def shifted(slot, units, _):
            for unit in units:
                query_frame, keys = frames_at(slot, unit)
                scores = scores_of(slot, unit) + bias_of(unit)
                old = top_ref[query_frame]
                new = jnp.maximum(old, jnp.max(scores, axis=1, keepdims=True))
                keep = by_head(jnp.exp(old - new))
                weights = jnp.exp(scores - new[:, :1])
                sum_ref[query_frame] = sum_ref[query_frame] * keep + sums_of(keys, weights)
                total_ref[query_frame] = total_ref[query_frame] * keep + totals_of(weights)
                top_ref[query_frame] = new

        fetch(0, 0)
        over_blocks(0, len(sources) * per_source, shifted)
        lax.fori_loop(0, query_frames, gather_totals, 0)

    for index, out_ref in enumerate(out_refs):

        def finish(frame, carry):
            here = index * frames_here + frame
            out_ref[frame] = (sum_ref[here] / whole_ref[here]).astype(out_ref.dtype)
            return carry

        lax.fori_loop(0, frames_here, finish, 0, unroll=4)


def attend(queries, chunks, pairs, table, places, order, begin, number, group, state, ends):
    frames_here = queries[0].shape[0]
    shape = (len(chunks) * frames_here, TOKF, LANES)
    held = jax.ShapeDtypeStruct(shape, jnp.float32)
    whole = pl.BlockSpec(memory_space=pltpu.VMEM)
    scalars = pl.BlockSpec(memory_space=pltpu.SMEM)
    stays = pl.BlockSpec(memory_space=pltpu.HBM)
    room = pltpu.VMEM(shape, jnp.float32)
    wide = (shape[0], PACKED, LANES)
    common = [
        pltpu.VMEM((2, group) + pairs[0][0].shape[1:], queries[0].dtype),
        pltpu.VMEM(wide, queries[0].dtype),
        pltpu.VMEM((len(chunks),) + queries[0].shape, queries[0].dtype),
        pltpu.VMEM((UNROLL, PACKED, PACKED), jnp.float32),
        pltpu.SemaphoreType.DMA((2 + len(chunks),)),
        pltpu.SemaphoreType.DMA((len(chunks),)),
    ]
    listed = [array for plane in pairs for array in plane] + [array for pair in state for array in pair]
    return pl.pallas_call(
        functools.partial(
            attend_kernel,
            begin,
            number,
            tuple(chunks),
            tuple(len(plane) for plane in pairs),
            len(state),
            ends,
        ),
        in_specs=[scalars, scalars] + [stays] * (1 + len(queries) + len(listed)),
        out_specs=[whole] + ([whole] * len(chunks) if ends else [stays, stays]),
        out_shape=[jax.ShapeDtypeStruct(order.shape, order.dtype)]
        + (
            [jax.ShapeDtypeStruct(query.shape, query.dtype) for query in queries]
            if ends
            else [held, held]
        ),
        scratch_shapes=[room] * 2
        + common
        + ([room, pltpu.VMEM(wide, jnp.float32)] if ends else []),
        compiler_params=pltpu.CompilerParams(vmem_limit_bytes=VMEM_LIMIT),
        cost_estimate=pl.CostEstimate(flops=1, bytes_accessed=1, transcendentals=0),
    )(table, places, order, *queries, *listed)


def project_kernel(parts, place_ref, near_ref, far_ref, *refs):
    plane, side = place_ref[0], place_ref[2]
    out_ref = refs[2 * parts]
    columns = out_ref.shape[1]
    mine = pl.ds(pl.multiple_of(side * columns, columns), columns)
    rows = [pl.ds(pl.multiple_of((plane ^ part) * LANES, LANES), LANES) for part in range(parts)]
    merged = jnp.concatenate([ref[...] for ref in refs[: 2 * parts]], axis=1)
    weight = [near_ref[row, mine] for row in rows] + [far_ref[row, :] for row in rows]
    out_ref[...] = jnp.dot(
        merged, jnp.concatenate(weight, axis=0), preferred_element_type=jnp.float32
    ).astype(out_ref.dtype)


def project(merged, others, near, far, places):
    rows = merged[0].shape[0]
    tile = rows // 4 if rows % 64 == 0 else rows
    parts = merged + others
    columns = far.shape[1]
    return pl.pallas_call(
        functools.partial(project_kernel, len(merged)),
        grid=(rows // tile,),
        in_specs=[pl.BlockSpec(memory_space=pltpu.SMEM)]
        + [pl.BlockSpec(weight.shape, lambda row: (0, 0)) for weight in (near, far)]
        + [pl.BlockSpec((tile, part.shape[1]), lambda row: (row, 0)) for part in parts],
        out_specs=pl.BlockSpec((tile, columns), lambda row: (row, 0)),
        out_shape=jax.ShapeDtypeStruct((rows, columns), parts[0].dtype),
        compiler_params=pltpu.CompilerParams(vmem_limit_bytes=VMEM_LIMIT),
        cost_estimate=pl.CostEstimate(
            flops=4 * rows * far.size, bytes_accessed=rows * 4096, transcendentals=0
        ),
    )(places, near, far, *parts)


def spread(queries, pairs, far, table, places, swap, across, gather, plane_size):
    chunk_order = [0, 3, 1, 2]
    barrier = lax.optimization_barrier
    order = jnp.zeros((8, LANES), jnp.int32)

    def run(distances, plane, keyed, state, ends=False, number=1):
        return attend(
            [queries[distance] for distance in distances],
            [chunk_order.index(distance) for distance in distances],
            keyed if ends else keyed[plane : plane + number],
            table,
            places,
            order,
            plane,
            number,
            plane_size,
            state,
            ends,
        )

    def gathered(distance):
        return [gather(pairs[distance], plane_size)]

    keyed = [gathered(0), None, None, None]
    queries[3], queries[1] = swap(queries[3], 3), swap(queries[1], 1)
    queries[3], queries[1], pairs[1], table, order = barrier(
        (queries[3], queries[1], pairs[1], table, order)
    )
    pairs[1] = swap(pairs[1], 1)
    pairs[1], pairs[3], far, order = barrier((pairs[1], pairs[3], far, order))
    keyed[1] = gathered(1)
    pairs[3], far = swap(pairs[3], 3), across(far)
    order, *state = run([0, 3, 1], 0, keyed, [])
    pairs[3], pairs[2], far, order = barrier((pairs[3], pairs[2], far, order))
    keyed[3] = gathered(3)
    pairs[2] = swap(pairs[2], 2)
    order, *state = run([0, 3, 1], 1, keyed, [state])
    pairs[2], queries[2], order = barrier((pairs[2], queries[2], order))
    keyed[2] = gathered(2)
    queries[2] = swap(queries[2], 2)
    order, *state = run([0, 3, 1], 3, keyed, [state])
    queries[2], order = barrier((queries[2], order))
    order, *last = run([2], 0, keyed, [], number=2)
    merged, others = [None] * 4, [None] * 4

    def rows_of(out):
        return out.reshape(-1, LANES)

    order, out = run([2], 2, keyed, [last], True, 2)
    out, order = barrier((rows_of(out), order))
    merged[2] = swap(out, 2)
    order, near_out, out = run([0, 3], 2, keyed, [state], True)
    merged[0], out, merged[2], order = barrier((rows_of(near_out), rows_of(out), merged[2], order))
    merged[3], others[0], others[2] = swap(out, 3), across(merged[0]), across(merged[2])
    order, out = run([1], 2, keyed, [state], True)
    out, merged[3], others[0], others[2] = barrier((rows_of(out), merged[3], others[0], others[2]))
    merged[1], others[3] = swap(out, 1), across(merged[3])
    others[1] = across(merged[1])
    return merged, others, far


def body(query_states, key_states, value_states, pair_list, out_weight):
    peers = lax.axis_size("frames")
    my_index = lax.axis_index("frames")
    rows, columns = query_states.shape
    frames_here = rows // TOKF
    planes = columns // LANES
    plane_size = peers // planes
    group = min(plane_size, GROUP)
    plane, place = my_index // plane_size, my_index % plane_size
    side = lax.axis_index("heads")
    places = jnp.stack([plane, place, side]).astype(jnp.int32)
    table = attend_table(pair_list, planes, plane_size, group, frames_here, places)
    per_plane = plane_size // group

    def swap(array, distance, axis=plane_size):
        if distance == 0:
            return array
        return lax.ppermute(
            array, "frames", [(index, index ^ (distance * axis)) for index in range(peers)]
        )

    def gather(array, size):
        members = [list(range(start, start + size)) for start in range(0, peers, size)]
        return lax.all_gather(array, "frames", axis_index_groups=members)

    def across(array):
        return lax.ppermute(array, "heads", [(0, 1), (1, 0)])

    def columns_of(array, distance):
        chosen = lax.dynamic_slice_in_dim(array, (plane ^ distance) * LANES, LANES, 1)
        return chosen.reshape(frames_here, TOKF, LANES)

    queries = [columns_of(query_states, distance) for distance in range(planes)]
    pairs = [
        jnp.stack([columns_of(key_states, distance), columns_of(value_states, distance)])
        for distance in range(planes)
    ]
    two = lax.axis_size("heads") == 2
    far = lax.dynamic_slice_in_dim(out_weight, (1 - side) * columns, columns, 1)
    if planes == 1:
        keyed = [[gather(pairs[0], plane_size)]]
        order = jnp.zeros((8, LANES), jnp.int32)
        _, out = attend(
            queries, [0], keyed, table, places, order, 0, per_plane, group, [], True
        )
        out = out.reshape(rows, LANES)
        if not two:
            term = jnp.dot(out, out_weight, preferred_element_type=jnp.float32)
            return lax.psum_scatter(
                term.astype(out.dtype), "heads", scatter_dimension=1, tiled=True
            )
        return project([out], [across(out)], out_weight, across(far), places)
    assert two
    merged, others, far = spread(
        queries, pairs, far, table, places, swap, across, gather, plane_size
    )
    return project(merged, others, out_weight, far, places)


def solution(mesh):
    placed = (
        P("frames", "heads"),
        P("frames", "heads"),
        P("frames", "heads"),
        P(),
        P("heads", None),
    )
    return jax.shard_map(
        body, mesh=mesh, in_specs=placed, out_specs=P("frames", "heads"), check_vma=False
    )
```

time: 1440 us -> 460 us (0.32); the launches traced: 1420 us -> 459 us
  local copies, waits for them, and re-layouts: 393 us -> 9.53 us
  Pallas kernels: 0 us -> 350 us
  blocking collectives: 279 us -> 0 us
  waiting for transfers between devices: 285 us -> 48.1 us
  matrix products: 230 us -> 0 us
  other arithmetic: 150 us -> 5.57 us
  starting transfers between devices: 72 us -> 32.2 us
    pallas_call x0 -> x9, Pallas kernels: none -> 350 us  [the longest x7 339 us: attend(): pl.pallas_call(functools.partial(attend_kernel, begin, number, tuple(chun...]
    all_to_all x1 -> x0, blocking collectives: 279 us -> none  [body(): lax.all_to_all(to_peers(pick_rows(frame_query, peer_frame, peer_live)), '...]
    dynamic_slice x170 -> x3, local copies, waits for them, and re-layouts: 258 us -> 5.03 us  [the longest x2 4.16 us: columns_of(): lax.dynamic_slice_in_dim(array, (plane ^ distance) * LANES, LANES, 1)]
    dot_general x71 -> x0, matrix products: 230 us -> none  [the longest x1 93.7 us: combine(): jnp.einsum('xf,xthd->fthd', member_float, weighted, precision=lax.Precisi...]
    all_to_all x4 -> x0, waiting for transfers between devices: 193 us -> none  [the longest x1 175 us: body(): lax.all_to_all(to_peers(pick_rows(frame_value, peer_frame, peer_live)), '...]
    reduce_scatter x1 -> x0, waiting for transfers between devices: 92.2 us -> none  [body(): lax.psum_scatter(head_term.astype(jnp.bfloat16), 'heads', scatter_dimensi...]
    all_to_all x4 -> x0, starting transfers between devices: 72 us -> none  [the longest x1 53.7 us: body(): lax.all_to_all(to_peers(pick_rows(frame_key, peer_frame, peer_live)), 'fr...]
    dynamic_update_slice x50 -> x0, local copies, waits for them, and re-layouts: 55.8 us -> none  [in_groups(): lax.map(lambda grouped: attend(grouped[0], grouped[1], grouped[2]), stacked)]
  transfers between devices with their start and end apart: 5 -> 18, of which waited for: 3 -> 6; matrix products, arithmetic and copies ran while one was open for 40% -> 1% of each run, Pallas kernels for 0% -> 60%
where the time goes in v1:
time: 460 us; the launch traced here: 459 us
  Pallas kernels  350 us (76%)
  waiting for transfers between devices  48.1 us (10%)
  starting transfers between devices  32.2 us (7%)
  between operations  13.4 us (3%)
  local copies, waits for them, and re-layouts  9.53 us (2%)
  other arithmetic  5.57 us (1%)
    pallas_call x7, Pallas kernels, attend(): pl.pallas_call(functools.partial(attend_kernel, begin, number, tuple(chun...  339 us
    ppermute x9, waiting for transfers between devices, swap(): lax.ppermute(array, 'frames', [(index, index ^ distance * axis) for index...  40.6 us
    ppermute x9, starting transfers between devices, swap(): lax.ppermute(array, 'frames', [(index, index ^ distance * axis) for index...  25.6 us
  transfers between devices with their start and end apart: 18, of which 6 were waited for; matrix products, arithmetic and copies ran while one was open for 1% of the time, Pallas kernels for 60%

profile of v1, /device:TPU:0, one launch (start us, length us, event | category | flops | bytes accessed | tf_op | source)
XLA Modules:
  0.0 459.2 jit_solution(15085440109509384002)
XLA Ops:
  6.5 2.6 constant_dynamic-slice_fusion.2
  9.1 1.6 constant_dynamic-slice_fusion
  10.7 0.9 pad_maximum_fusion.3
  11.7 0.0 all-gather.11.cloned.1.call-start
  11.7 5.1 %collective-permute-start = (bf16[8,192,128]{2,1,0:T(8,128)(2,1)}, bf16[8,192,128]{2,1,0:T(8,128)(2,1)S(1)}, u32[]{:S(2)}, u32[]{:S(2)}) collective-permute-start(bf16[8,192,128]{2,1,0:T(8,128)(2,1)} %bitcast.3), channel_id=1, source_target_pairs={{0,24},{2,26},{4,28},{6,30},{8,16},{10,18},{12,20},{14,22},{16,8},... | collective-permute-start | bytes 1179656 | tf_op jit(solution)/shard_map/ppermute | solution.py:552
  16.9 0.6 copy.8
  17.5 0.7 pad_add_fusion.place_ref
  18.1 5.6 %shard_map.55.table_ref = s32[4,2,256]{2,1,0:T(2,128)} custom-call(s32[3]{0:T(128)} %pad_add_fusion.place_ref, s32[2,8,128]{2,1,0:T(8,128)} %bitcast.61), custom_call_target="tpu_custom_call" | custom-call | tf_op jit(solution)/shard_map/pallas_call | solution.py:130
  23.7 2.0 pad_maximum_fusion
  25.7 1.4 collective-permute-done.refs_1_
  27.1 7.6 %collective-permute-done.1.refs_2_.refs_0_ = bf16[8,192,128]{2,1,0:T(8,128)(2,1)S(1)} collective-permute-done((bf16[8,192,128]{2,1,0:T(8,128)(2,1)}, bf16[8,192,128]{2,1,0:T(8,128)(2,1)S(1)}, u32[]{:S(2)}, u32[]{:S(2)}) %collective-permute-start.1) | collective-permute-done | bytes 393248 | tf_op jit(solution)/shard_map/ppermute | solution.py:552
  34.7 1.7 collective-permute-start.2
  36.4 0.9 constant_dynamic-slice_fusion.6
  37.3 1.9 pad_maximum_fusion.1
  39.2 15.4 %collective-permute-done.2 = bf16[2,8,192,128]{3,2,1,0:T(8,128)(2,1)} collective-permute-done((bf16[2,8,192,128]{3,2,1,0:T(8,128)(2,1)}, bf16[2,8,192,128]{3,2,1,0:T(8,128)(2,1)}, u32[]{:S(2)}, u32[]{:S(2)}) %collective-permute-start.2) | collective-permute-done | bytes 786464 | tf_op jit(solution)/shard_map/ppermute | solution.py:552
  54.6 0.0 all-gather.13.cloned.1.call-start
  54.7 0.7 collective-permute-start.3
  55.4 1.3 collective-permute-start.4
  56.7 0.1 pad_maximum_fusion.2
  56.8 0.0 all-gather.9.cloned.1.call-done
  56.9 0.6 broadcast_in_dim.3.order_ref
  57.5 21.1 %shard_map.56 = (s32[8,128]{1,0:T(8,128)}, f32[24,192,128]{2,1,0:T(8,128)}, f32[24,192,128]{2,1,0:T(8,128)}) custom-call(s32[4,2,256]{2,1,0:T(2,128)} %shard_map.55.table_ref, s32[3]{0:T(128)} %pad_add_fusion.place_ref, s32[8,128]{1,0:T(8,128)} %broadcast_in_dim.3.order_ref, bf16[8,192,128]{2,1,0:T(8,128)(2,1)} %bitcast.45, bf16[8,192,128]{2,1,0:T(8,128)(2,1)} %copy-done.1, ...), custom_call_target="tpu_custom_call" | custom-call | flops 1 | bytes 1 | tf_op jit(solution)/shard_map/pallas_call | solution.py:415
  78.6 0.9 copy-done.6
  79.5 0.0 all-gather.15.cloned.1.call-start
  79.5 11.3 %collective-permute-start.5 = (bf16[2,8,192,128]{3,2,1,0:T(8,128)(2,1)S(1)}, bf16[2,8,192,128]{3,2,1,0:T(8,128)(2,1)S(1)}, u32[]{:S(2)}, u32[]{:S(2)}) collective-permute-start(bf16[2,8,192,128]{3,2,1,0:T(8,128)(2,1)S(1)} %pad_maximum_fusion.2), channel_id=1, source_target_pairs={{0,16},{2,18},{4,20},{6,22},{8,24},{10,26},{12,28},{14,30},{16,0},... | collective-permute-start | bytes 2359304 | tf_op jit(solution)/shard_map/ppermute | solution.py:552
  90.9 23.0 %shard_map.57 = (s32[8,128]{1,0:T(8,128)}, f32[24,192,128]{2,1,0:T(8,128)}, f32[24,192,128]{2,1,0:T(8,128)}) custom-call(s32[4,2,256]{2,1,0:T(2,128)} %shard_map.55.table_ref, s32[3]{0:T(128)} %pad_add_fusion.place_ref, s32[8,128]{1,0:T(8,128)} %get-tuple-element.62.order_ref, bf16[8,192,128]{2,1,0:T(8,128)(2,1)} %bitcast.46, ...), custom_call_target="tpu_custom_call" | custom-call | flops 1 | bytes 1 | tf_op jit(solution)/shard_map/pallas_call | solution.py:415
  113.9 9.6 %collective-permute-done.5 = bf16[2,8,192,128]{3,2,1,0:T(8,128)(2,1)S(1)} collective-permute-done((bf16[2,8,192,128]{3,2,1,0:T(8,128)(2,1)S(1)}, bf16[2,8,192,128]{3,2,1,0:T(8,128)(2,1)S(1)}, u32[]{:S(2)}, u32[]{:S(2)}) %collective-permute-start.5) | collective-permute-done | bytes 786464 | tf_op jit(solution)/shard_map/ppermute | solution.py:552
  123.5 0.9 copy-done.7
  124.4 0.1 collective-permute-start.6
  124.5 0.0 all-gather.13.cloned.1.call-done
  124.5 22.9 %shard_map.58 = (s32[8,128]{1,0:T(8,128)}, f32[24,192,128]{2,1,0:T(8,128)}, f32[24,192,128]{2,1,0:T(8,128)}) custom-call(s32[4,2,256]{2,1,0:T(2,128)} %shard_map.55.table_ref, s32[3]{0:T(128)} %pad_add_fusion.place_ref, s32[8,128]{1,0:T(8,128)} %get-tuple-element.68.order_ref, bf16[8,192,128]{2,1,0:T(8,128)(2,1)} %bitcast.47, ...), custom_call_target="tpu_custom_call" | custom-call | flops 1 | bytes 1 | tf_op jit(solution)/shard_map/pallas_call | solution.py:415
  147.5 0.7 copy-done.5
  148.2 14.8 %shard_map.59 = (s32[8,128]{1,0:T(8,128)}, f32[8,192,128]{2,1,0:T(8,128)}, f32[8,192,128]{2,1,0:T(8,128)}) custom-call(s32[4,2,256]{2,1,0:T(2,128)} %shard_map.55.table_ref, s32[3]{0:T(128)} %pad_add_fusion.place_ref, s32[8,128]{1,0:T(8,128)} %get-tuple-element.73.order_ref, bf16[8,192,128]{2,1,0:T(8,128)(2,1)} %copy-done.5, ...), custom_call_target="tpu_custom_call" | custom-call | flops 1 | bytes 1 | tf_op jit(solution)/shard_map/pallas_call | solution.py:415
  163.0 0.0 all-gather.15.cloned.1.call-done
  163.1 71.0 %shard_map.60 = (s32[8,128]{1,0:T(8,128)}, bf16[8,192,128]{2,1,0:T(8,128)(2,1)}) custom-call(s32[4,2,256]{2,1,0:T(2,128)} %shard_map.55.table_ref, s32[3]{0:T(128)} %pad_add_fusion.place_ref, s32[8,128]{1,0:T(8,128)} %get-tuple-element.75.order_ref, bf16[8,192,128]{2,1,0:T(8,128)(2,1)} %copy-done.5, bf16[4,2,8,192,128]{4,3,2,1,0:T(8,128)(2,1)} %bitcast.30, ...), custom_call_target="tpu_custom_call" | custom-call | flops 1 | bytes 1 | tf_op jit(solution)/shard_map/pallas_call | solution.py:415
  234.0 4.2 collective-permute-start.7
  238.3 123.3 %shard_map.61 = (s32[8,128]{1,0:T(8,128)}, bf16[8,192,128]{2,1,0:T(8,128)(2,1)}, bf16[8,192,128]{2,1,0:T(8,128)(2,1)}) custom-call(s32[4,2,256]{2,1,0:T(2,128)} %shard_map.55.table_ref, s32[3]{0:T(128)} %pad_add_fusion.place_ref, s32[8,128]{1,0:T(8,128)} %get-tuple-element.81.order_ref, bf16[8,192,128]{2,1,0:T(8,128)(2,1)} %bitcast.48, ...), custom_call_target="tpu_custom_call" | custom-call | flops 1 | bytes 1 | tf_op jit(solution)/shard_map/pallas_call | solution.py:415
  361.7 0.1 collective-permute-start.8
  361.7 1.6 collective-permute-start.9
  363.3 0.5 collective-permute-start.10
  363.8 62.9 %shard_map.62 = (s32[8,128]{1,0:T(8,128)}, bf16[8,192,128]{2,1,0:T(8,128)(2,1)}) custom-call(s32[4,2,256]{2,1,0:T(2,128)} %shard_map.55.table_ref, s32[3]{0:T(128)} %pad_add_fusion.place_ref, s32[8,128]{1,0:T(8,128)} %get-tuple-element.89.order_ref, bf16[8,192,128]{2,1,0:T(8,128)(2,1)} %copy-done, bf16[4,2,8,192,128]{4,3,2,1,0:T(8,128)(2,1)} %bitcast.32, ...), custom_call_target="tpu_custom_call" | custom-call | flops 1 | bytes 1 | tf_op jit(solution)/shard_map/pallas_call | solution.py:415
  426.8 2.4 collective-permute-start.11
  429.2 1.5 collective-permute-start.13
  430.7 6.5 %collective-permute-done.11.refs_1_ = bf16[1536,128]{1,0:T(8,128)(2,1)S(1)} collective-permute-done((bf16[1536,128]{1,0:T(8,128)(2,1)}, bf16[1536,128]{1,0:T(8,128)(2,1)S(1)}, u32[]{:S(2)}, u32[]{:S(2)}) %collective-permute-start.11) | collective-permute-done | bytes 393248 | tf_op jit(solution)/shard_map/ppermute | solution.py:552
  437.2 1.5 collective-permute-start.12
  438.7 7.4 %collective-permute-done.12.refs_5_ = bf16[1536,128]{1,0:T(8,128)(2,1)S(1)} collective-permute-done((bf16[1536,128]{1,0:T(8,128)(2,1)S(1)}, bf16[1536,128]{1,0:T(8,128)(2,1)S(1)}, u32[]{:S(2)}, u32[]{:S(2)}) %collective-permute-start.12) | collective-permute-done | bytes 393248 | tf_op jit(solution)/shard_map/ppermute | solution.py:561
  446.2 0.7 copy-done.15
  446.9 5.7 %shard_map.63 = bf16[1536,512]{1,0:T(8,128)(2,1)} custom-call(s32[3]{0:T(128)} %pad_add_fusion.place_ref, bf16[512,1024]{1,0:T(8,128)(2,1)} %near_ref.1, bf16[512,512]{1,0:T(8,128)(2,1)} %collective-permute-done.4.far_ref, bf16[1536,128]{1,0:T(8,128)(2,1)} %bitcast.59, bf16[1536,128]{1,0:T(8,128)(2,1)} %copy-done.13, bf16[1536,128]{1,0:T(8,128)(2,1)} %copy-done.9, ...), custom_call_target="tpu_custom_call" | custom-call | flops 1610612736 | bytes 6291456 | tf_op jit(solution)/shard_map/pallas_call | solution.py:459
  (45 shorter events, 0.2 us)
Async XLA Ops:
  6.5 2.6 copy-start.3
  6.5 50.3 %all-gather.9.cloned.1.call-start = ((), (), s32[]{:S(2)}) async-start(), calls=%async_computation | async-start | bytes 3932160 | tf_op jit(solution)/shard_map/all_gather | solution.py:558
  6.5 2.6 copy-start.4
  10.7 6.1 %copy-start.16 = (s32[1024,2]{0,1:T(2,128)S(1)}, s32[1024,2]{0,1:T(2,128)}, u32[]{:S(2)}) copy-start(s32[1024,2]{0,1:T(2,128)} %param.8) | copy-start | bytes 24580
  10.7 25.7 %copy-start.2 = (bf16[512,1024]{1,0:T(8,128)(2,1)S(1)}, bf16[512,1024]{1,0:T(8,128)(2,1)}, u32[]{:S(2)}) copy-start(bf16[512,1024]{1,0:T(8,128)(2,1)} %near_ref.1) | copy-start | bytes 3145732
  11.7 79.2 %all-gather.11.cloned.1.call-start = ((), (), s32[]{:S(2)}) async-start(), calls=%async_computation.1 | async-start | bytes 3932160 | tf_op jit(solution)/shard_map/all_gather | solution.py:558
  11.7 15.4 %collective-permute-start = (bf16[8,192,128]{2,1,0:T(8,128)(2,1)}, bf16[8,192,128]{2,1,0:T(8,128)(2,1)S(1)}, u32[]{:S(2)}, u32[]{:S(2)}) collective-permute-start(bf16[8,192,128]{2,1,0:T(8,128)(2,1)} %bitcast.3), channel_id=1, source_target_pairs={{0,24},{2,26},{4,28},{6,30},{8,16},{10,18},{12,20},{14,22},{16,8},... | collective-permute-start | bytes 1179656 | tf_op jit(solution)/shard_map/ppermute | solution.py:552
  16.9 17.9 %collective-permute-start.1 = (bf16[8,192,128]{2,1,0:T(8,128)(2,1)}, bf16[8,192,128]{2,1,0:T(8,128)(2,1)S(1)}, u32[]{:S(2)}, u32[]{:S(2)}) collective-permute-start(bf16[8,192,128]{2,1,0:T(8,128)(2,1)} %bitcast.60), channel_id=1, source_target_pairs={{0,8},{2,10},{4,12},{6,14},{8,0},{10,2},{12,4},{14,6},{16,24},{18,... | collective-permute-start | bytes 1179656 | tf_op jit(solution)/shard_map/ppermute | solution.py:552
  27.1 29.7 %copy-start.1 = (bf16[8,192,128]{2,1,0:T(8,128)(2,1)}, bf16[8,192,128]{2,1,0:T(8,128)(2,1)S(1)}, u32[]{:S(2)}) copy-start(bf16[8,192,128]{2,1,0:T(8,128)(2,1)S(1)} %collective-permute-done.refs_1_) | copy-start | bytes 1179652
  34.7 22.1 %copy-start = (bf16[8,192,128]{2,1,0:T(8,128)(2,1)}, bf16[8,192,128]{2,1,0:T(8,128)(2,1)S(1)}, u32[]{:S(2)}) copy-start(bf16[8,192,128]{2,1,0:T(8,128)(2,1)S(1)} %collective-permute-done.1.refs_2_.refs_0_) | copy-start | bytes 1179652
  34.7 19.9 %collective-permute-start.2 = (bf16[2,8,192,128]{3,2,1,0:T(8,128)(2,1)}, bf16[2,8,192,128]{3,2,1,0:T(8,128)(2,1)}, u32[]{:S(2)}, u32[]{:S(2)}) collective-permute-start(bf16[2,8,192,128]{3,2,1,0:T(8,128)(2,1)} %pad_maximum_fusion), channel_id=1, source_target_pairs={{0,8},{2,10},{4,12},{6,14},{8,0},{10,2},{12,4},{14,6},{16,24},{18,... | collective-permute-start | bytes 2359304 | tf_op jit(solution)/shard_map/ppermute | solution.py:552
  54.6 69.9 %all-gather.13.cloned.1.call-start = ((), (), s32[]{:S(2)}) async-start(), calls=%async_computation.2 | async-start | bytes 3932160 | tf_op jit(solution)/shard_map/all_gather | solution.py:558
  54.7 23.9 %collective-permute-start.3 = (bf16[2,8,192,128]{3,2,1,0:T(8,128)(2,1)}, bf16[2,8,192,128]{3,2,1,0:T(8,128)(2,1)S(1)}, u32[]{:S(2)}, u32[]{:S(2)}) collective-permute-start(bf16[2,8,192,128]{3,2,1,0:T(8,128)(2,1)} %pad_maximum_fusion.1), channel_id=1, source_target_pairs={{0,24},{2,26},{4,28},{6,30},{8,16},{10,18},{12,20},{14,22},{16,8},... | collective-permute-start | bytes 2359304 | tf_op jit(solution)/shard_map/ppermute | solution.py:552
  55.4 23.1 %collective-permute-start.4 = (bf16[512,512]{1,0:T(8,128)(2,1)}, bf16[512,512]{1,0:T(8,128)(2,1)}, u32[]{:S(2)}, u32[]{:S(2)}) collective-permute-start(bf16[512,512]{1,0:T(8,128)(2,1)} %constant_dynamic-slice_fusion.6), channel_id=1, source_target_pairs={{0,1},{1,0},{2,3},{3,2},{4,5},{5,4},{6,7},{7,6},{8,9},{9,8},{10,11... | collective-permute-start | bytes 1572872 | tf_op jit(solution)/shard_map/ppermute | solution.py:561
  78.6 0.9 copy-start.6
  79.5 83.6 %all-gather.15.cloned.1.call-start = ((), (), s32[]{:S(2)}) async-start(), calls=%async_computation.3 | async-start | bytes 3932160 | tf_op jit(solution)/shard_map/all_gather | solution.py:558
  79.5 44.0 %collective-permute-start.5 = (bf16[2,8,192,128]{3,2,1,0:T(8,128)(2,1)S(1)}, bf16[2,8,192,128]{3,2,1,0:T(8,128)(2,1)S(1)}, u32[]{:S(2)}, u32[]{:S(2)}) collective-permute-start(bf16[2,8,192,128]{3,2,1,0:T(8,128)(2,1)S(1)} %pad_maximum_fusion.2), channel_id=1, source_target_pairs={{0,16},{2,18},{4,20},{6,22},{8,24},{10,26},{12,28},{14,30},{16,0},... | collective-permute-start | bytes 2359304 | tf_op jit(solution)/shard_map/ppermute | solution.py:552
  90.9 33.6 %copy-start.8 = (bf16[1536,128]{1,0:T(8,128)(2,1)S(1)}, bf16[1536,128]{1,0:T(8,128)(2,1)}, u32[]{:S(2)}) copy-start(bf16[1536,128]{1,0:T(8,128)(2,1)} %get-tuple-element.97) | copy-start | bytes 1179652
  123.5 0.9 copy-start.7
  124.4 23.1 %collective-permute-start.6 = (bf16[8,192,128]{2,1,0:T(8,128)(2,1)S(1)}, bf16[8,192,128]{2,1,0:T(8,128)(2,1)S(1)}, u32[]{:S(2)}, u32[]{:S(2)}) collective-permute-start(bf16[8,192,128]{2,1,0:T(8,128)(2,1)S(1)} %bitcast.57), channel_id=1, source_target_pairs={{0,16},{2,18},{4,20},{6,22},{8,24},{10,26},{12,28},{14,30},{16,0},... | collective-permute-start | bytes 1179656 | tf_op jit(solution)/shard_map/ppermute | solution.py:552
  147.5 0.8 copy-start.5
  234.0 127.6 %collective-permute-start.7 = (bf16[1536,128]{1,0:T(8,128)(2,1)}, bf16[1536,128]{1,0:T(8,128)(2,1)S(1)}, u32[]{:S(2)}, u32[]{:S(2)}) collective-permute-start(bf16[1536,128]{1,0:T(8,128)(2,1)} %bitcast.65), channel_id=1, source_target_pairs={{0,16},{2,18},{4,20},{6,22},{8,24},{10,26},{12,28},{14,30},{16,0},... | collective-permute-start | bytes 1179656 | tf_op jit(solution)/shard_map/ppermute | solution.py:552
  361.7 65.1 %copy-start.9 = (bf16[1536,128]{1,0:T(8,128)(2,1)}, bf16[1536,128]{1,0:T(8,128)(2,1)S(1)}, u32[]{:S(2)}) copy-start(bf16[1536,128]{1,0:T(8,128)(2,1)S(1)} %collective-permute-done.7.refs_2_) | copy-start | bytes 1179652
  361.7 65.1 %collective-permute-start.8 = (bf16[1536,128]{1,0:T(8,128)(2,1)}, bf16[1536,128]{1,0:T(8,128)(2,1)S(1)}, u32[]{:S(2)}, u32[]{:S(2)}) collective-permute-start(bf16[1536,128]{1,0:T(8,128)(2,1)} %bitcast.63), channel_id=1, source_target_pairs={{0,24},{2,26},{4,28},{6,30},{8,16},{10,18},{12,20},{14,22},{16,8},... | collective-permute-start | bytes 1179656 | tf_op jit(solution)/shard_map/ppermute | solution.py:552
  361.7 65.0 %collective-permute-start.9 = (bf16[1536,128]{1,0:T(8,128)(2,1)}, bf16[1536,128]{1,0:T(8,128)(2,1)S(1)}, u32[]{:S(2)}, u32[]{:S(2)}) collective-permute-start(bf16[1536,128]{1,0:T(8,128)(2,1)} %bitcast.58), channel_id=1, source_target_pairs={{0,1},{1,0},{2,3},{3,2},{4,5},{5,4},{6,7},{7,6},{8,9},{9,8},{10,11... | collective-permute-start | bytes 1179656 | tf_op jit(solution)/shard_map/ppermute | solution.py:561
  363.3 63.4 %collective-permute-start.10 = (bf16[1536,128]{1,0:T(8,128)(2,1)S(1)}, bf16[1536,128]{1,0:T(8,128)(2,1)S(1)}, u32[]{:S(2)}, u32[]{:S(2)}) collective-permute-start(bf16[1536,128]{1,0:T(8,128)(2,1)S(1)} %collective-permute-done.7.refs_2_), channel_id=1, source_target_pairs={{0,1},{1,0},{2,3},{3,2},{4,5},{5,4},{6,7},{7,6},{8,9},{9,8},{10,11... | collective-permute-start | bytes 1179656 | tf_op jit(solution)/shard_map/ppermute | solution.py:561
  426.7 19.4 %copy-start.10 = (bf16[1536,128]{1,0:T(8,128)(2,1)}, bf16[1536,128]{1,0:T(8,128)(2,1)S(1)}, u32[]{:S(2)}) copy-start(bf16[1536,128]{1,0:T(8,128)(2,1)S(1)} %collective-permute-done.8.refs_3_) | copy-start | bytes 1179652
  426.8 19.3 %copy-start.11 = (bf16[1536,128]{1,0:T(8,128)(2,1)}, bf16[1536,128]{1,0:T(8,128)(2,1)S(1)}, u32[]{:S(2)}) copy-start(bf16[1536,128]{1,0:T(8,128)(2,1)S(1)} %collective-permute-done.9.refs_4_) | copy-start | bytes 1179652
  426.8 19.3 %copy-start.12 = (bf16[1536,128]{1,0:T(8,128)(2,1)}, bf16[1536,128]{1,0:T(8,128)(2,1)S(1)}, u32[]{:S(2)}) copy-start(bf16[1536,128]{1,0:T(8,128)(2,1)S(1)} %collective-permute-done.10.refs_6_) | copy-start | bytes 1179652
  426.8 10.4 %collective-permute-start.11 = (bf16[1536,128]{1,0:T(8,128)(2,1)}, bf16[1536,128]{1,0:T(8,128)(2,1)S(1)}, u32[]{:S(2)}, u32[]{:S(2)}) collective-permute-start(bf16[1536,128]{1,0:T(8,128)(2,1)} %bitcast.64), channel_id=1, source_target_pairs={{0,8},{2,10},{4,12},{6,14},{8,0},{10,2},{12,4},{14,6},{16,24},{18,... | collective-permute-start | bytes 1179656 | tf_op jit(solution)/shard_map/ppermute | solution.py:552
  429.2 9.5 %collective-permute-start.13 = (bf16[1536,128]{1,0:T(8,128)(2,1)S(1)}, bf16[1536,128]{1,0:T(8,128)(2,1)S(1)}, u32[]{:S(2)}, u32[]{:S(2)}) collective-permute-start(bf16[1536,128]{1,0:T(8,128)(2,1)S(1)} %collective-permute-done.8.refs_3_), channel_id=1, source_target_pairs={{0,1},{1,0},{2,3},{3,2},{4,5},{5,4},{6,7},{7,6},{8,9},{9,8},{10,11... | collective-permute-start | bytes 1179656 | tf_op jit(solution)/shard_map/ppermute | solution.py:561
  437.2 8.9 %copy-start.13 = (bf16[1536,128]{1,0:T(8,128)(2,1)}, bf16[1536,128]{1,0:T(8,128)(2,1)S(1)}, u32[]{:S(2)}) copy-start(bf16[1536,128]{1,0:T(8,128)(2,1)S(1)} %collective-permute-done.11.refs_1_) | copy-start | bytes 1179652
  437.2 8.9 %collective-permute-start.12 = (bf16[1536,128]{1,0:T(8,128)(2,1)S(1)}, bf16[1536,128]{1,0:T(8,128)(2,1)S(1)}, u32[]{:S(2)}, u32[]{:S(2)}) collective-permute-start(bf16[1536,128]{1,0:T(8,128)(2,1)S(1)} %collective-permute-done.11.refs_1_), channel_id=1, source_target_pairs={{0,1},{1,0},{2,3},{3,2},{4,5},{5,4},{6,7},{7,6},{8,9},{9,8},{10,11... | collective-permute-start | bytes 1179656 | tf_op jit(solution)/shard_map/ppermute | solution.py:561
  438.7 7.4 %copy-start.14 = (bf16[1536,128]{1,0:T(8,128)(2,1)}, bf16[1536,128]{1,0:T(8,128)(2,1)S(1)}, u32[]{:S(2)}) copy-start(bf16[1536,128]{1,0:T(8,128)(2,1)S(1)} %collective-permute-done.13.refs_7_) | copy-start | bytes 1179652
  446.1 0.8 copy-start.15
Sparse Core Ops, SparseCore 0:
  11.8 31.2 all-gather.8
  54.7 26.8 all-gather.10
  83.2 34.1 all-gather.12
  124.5 28.0 all-gather.14

commit v2 on v1

--- a/solution.py
+++ b/solution.py
@@ -495,20 +495,21 @@
         return [gather(pairs[distance], plane_size)]
 
     keyed = [gathered(0), None, None, None]
-    queries[3], queries[1] = swap(queries[3], 3), swap(queries[1], 1)
-    queries[3], queries[1], pairs[1], table, order = barrier(
-        (queries[3], queries[1], pairs[1], table, order)
+    pairs[1], asked = swap(pairs[1], 1), swap(jnp.stack([queries[3], pairs[3][0]]), 3)
+    pairs[1], asked, valued, queries[1], table = barrier(
+        (pairs[1], asked, pairs[3][1], queries[1], table)
     )
-    pairs[1] = swap(pairs[1], 1)
-    pairs[1], pairs[3], far, order = barrier((pairs[1], pairs[3], far, order))
     keyed[1] = gathered(1)
-    pairs[3], far = swap(pairs[3], 3), across(far)
+    valued, queries[1] = swap(valued, 3), swap(queries[1], 1)
+    valued, asked, queries[1], pairs[2], far, order = barrier(
+        (valued, asked, queries[1], pairs[2], far, order)
+    )
+    queries[3], pairs[3] = asked[0], jnp.stack([asked[1], valued])
+    keyed[3] = gathered(3)
+    pairs[2], far = swap(pairs[2], 2), across(far)
     order, *state = run([0, 3, 1], 0, keyed, [])
-    pairs[3], pairs[2], far, order = barrier((pairs[3], pairs[2], far, order))
-    keyed[3] = gathered(3)
-    pairs[2] = swap(pairs[2], 2)
     order, *state = run([0, 3, 1], 1, keyed, [state])
-    pairs[2], queries[2], order = barrier((pairs[2], queries[2], order))
+    pairs[2], queries[2], far, order = barrier((pairs[2], queries[2], far, order))
     keyed[2] = gathered(2)
     queries[2] = swap(queries[2], 2)
     order, *state = run([0, 3, 1], 3, keyed, [state])
@@ -519,16 +520,15 @@
     def rows_of(out):
         return out.reshape(-1, LANES)
 
+    order, out, near_out = run([3, 1], 2, keyed, [state], True)
+    out, near_out, order = barrier((rows_of(out), rows_of(near_out), order))
+    merged[3], merged[1] = swap(out, 3), swap(near_out, 1)
     order, out = run([2], 2, keyed, [last], True, 2)
-    out, order = barrier((rows_of(out), order))
-    merged[2] = swap(out, 2)
-    order, near_out, out = run([0, 3], 2, keyed, [state], True)
-    merged[0], out, merged[2], order = barrier((rows_of(near_out), rows_of(out), merged[2], order))
-    merged[3], others[0], others[2] = swap(out, 3), across(merged[0]), across(merged[2])
-    order, out = run([1], 2, keyed, [state], True)
-    out, merged[3], others[0], others[2] = barrier((rows_of(out), merged[3], others[0], others[2]))
-    merged[1], others[3] = swap(out, 1), across(merged[3])
-    others[1] = across(merged[1])
+    out, merged[3], merged[1], order = barrier((rows_of(out), merged[3], merged[1], order))
+    merged[2], others[3], others[1] = swap(out, 2), across(merged[3]), across(merged[1])
+    order, out = run([0], 2, keyed, [state], True)
+    merged[0], others[3] = barrier((rows_of(out), others[3]))
+    others[0], others[2] = across(merged[0]), across(merged[2])
     return merged, others, far
 
 

time: 460 us -> 468 us (1.017)
  waiting for transfers between devices: 48.1 us -> 52.8 us
    ppermute x5, waiting for transfers between devices: 7.42 us -> 21.6 us  [across(): return lax.ppermute(array, 'heads', [(0, 1), (1, 0)])]
    ppermute x9, waiting for transfers between devices: 40.6 us -> 31.1 us  [swap(): lax.ppermute(array, 'frames', [(index, index ^ distance * axis) for index...]
  transfers between devices with their start and end apart: 18 -> 18, of which waited for: 6 -> 7; matrix products, arithmetic and copies ran while one was open for 1% -> 2% of each run, Pallas kernels for 60% -> 48%
where the time goes in v2:
time: 468 us; the launch traced here: 467 us
  Pallas kernels  352 us (75%)
  waiting for transfers between devices  52.8 us (11%)
  starting transfers between devices  32.8 us (7%)
  between operations  13.4 us (3%)
  local copies, waits for them, and re-layouts  11.1 us (2%)
  other arithmetic  5.52 us (1%)
    pallas_call x7, Pallas kernels, attend(): pl.pallas_call(functools.partial(attend_kernel, begin, number, tuple(chun...  340 us
    ppermute x9, waiting for transfers between devices, swap(): lax.ppermute(array, 'frames', [(index, index ^ distance * axis) for index...  31.1 us
    ppermute x9, starting transfers between devices, swap(): lax.ppermute(array, 'frames', [(index, index ^ distance * axis) for index...  27 us
    ppermute x5, waiting for transfers between devices, across(): return lax.ppermute(array, 'heads', [(0, 1), (1, 0)])  21.6 us
  transfers between devices with their start and end apart: 18, of which 7 were waited for; matrix products, arithmetic and copies ran while one was open for 2% of the time, Pallas kernels for 48%

profile of v2, /device:TPU:0, one launch (start us, length us, event | category | flops | bytes accessed | tf_op | source)
XLA Modules:
  0.0 467.4 jit_solution(1837120136276014400)
XLA Ops:
  6.5 2.9 constant_dynamic-slice_fusion
  9.4 1.0 pad_maximum_fusion.3
  10.4 0.0 all-gather.11.cloned.1.call-start
  10.5 1.0 pad_maximum_fusion
  11.5 3.0 collective-permute-start
  14.5 2.4 constant_dynamic-slice_fusion.2
  17.0 0.9 pad_maximum_fusion.1
  17.9 2.5 collective-permute-start.1
  20.4 0.6 copy.8
  21.0 0.6 pad_add_fusion.place_ref
  21.6 5.6 %shard_map.55.table_ref = s32[4,2,256]{2,1,0:T(2,128)} custom-call(s32[3]{0:T(128)} %pad_add_fusion.place_ref, s32[2,8,128]{2,1,0:T(8,128)} %bitcast.63), custom_call_target="tpu_custom_call" | custom-call | tf_op jit(solution)/shard_map/pallas_call | solution.py:130
  27.2 5.6 %collective-permute-done = bf16[2,8,192,128]{3,2,1,0:T(8,128)(2,1)S(1)} collective-permute-done((bf16[2,8,192,128]{3,2,1,0:T(8,128)(2,1)}, bf16[2,8,192,128]{3,2,1,0:T(8,128)(2,1)S(1)}, u32[]{:S(2)}, u32[]{:S(2)}) %collective-permute-start) | collective-permute-done | bytes 786464 | tf_op jit(solution)/shard_map/ppermute | solution.py:552
  32.8 18.7 %collective-permute-done.1 = bf16[2,8,192,128]{3,2,1,0:T(8,128)(2,1)} collective-permute-done((bf16[2,8,192,128]{3,2,1,0:T(8,128)(2,1)}, bf16[2,8,192,128]{3,2,1,0:T(8,128)(2,1)}, u32[]{:S(2)}, u32[]{:S(2)}) %collective-permute-start.1) | collective-permute-done | bytes 786464 | tf_op jit(solution)/shard_map/ppermute | solution.py:552
  51.6 0.0 all-gather.13.cloned.1.call-start
  51.6 2.3 collective-permute-start.2
  54.0 11.3 %collective-permute-start.3 = (bf16[8,192,128]{2,1,0:T(8,128)(2,1)}, bf16[8,192,128]{2,1,0:T(8,128)(2,1)S(1)}, u32[]{:S(2)}, u32[]{:S(2)}) collective-permute-start(bf16[8,192,128]{2,1,0:T(8,128)(2,1)} %bitcast.8), channel_id=1, source_target_pairs={{0,8},{2,10},{4,12},{6,14},{8,0},{10,2},{12,4},{14,6},{16,24},{18,... | collective-permute-start | bytes 1179656 | tf_op jit(solution)/shard_map/ppermute | solution.py:552
  65.3 0.1 pad_maximum_fusion.2
  65.3 0.5 collective-permute-done.2
  65.9 6.1 %collective-permute-done.3.refs_2_.refs_1_ = bf16[8,192,128]{2,1,0:T(8,128)(2,1)S(1)} collective-permute-done((bf16[8,192,128]{2,1,0:T(8,128)(2,1)}, bf16[8,192,128]{2,1,0:T(8,128)(2,1)S(1)}, u32[]{:S(2)}, u32[]{:S(2)}) %collective-permute-start.3) | collective-permute-done | bytes 393248 | tf_op jit(solution)/shard_map/ppermute | solution.py:552
  72.0 2.1 fusion
  74.1 1.9 pad_maximum_fusion.4
  76.1 0.0 all-gather.15.cloned.1.call-start
  76.1 1.6 collective-permute-start.4
  77.8 1.5 collective-permute-start.5
  79.3 0.6 broadcast_in_dim.3.order_ref
  79.9 21.2 %shard_map.56 = (s32[8,128]{1,0:T(8,128)}, f32[24,192,128]{2,1,0:T(8,128)}, f32[24,192,128]{2,1,0:T(8,128)}) custom-call(s32[4,2,256]{2,1,0:T(2,128)} %shard_map.55.table_ref, s32[3]{0:T(128)} %pad_add_fusion.place_ref, s32[8,128]{1,0:T(8,128)} %broadcast_in_dim.3.order_ref, bf16[8,192,128]{2,1,0:T(8,128)(2,1)} %bitcast.48, ...), custom_call_target="tpu_custom_call" | custom-call | flops 1 | bytes 1 | tf_op jit(solution)/shard_map/pallas_call | solution.py:415
  101.1 0.0 all-gather.11.cloned.1.call-done
  101.1 22.3 %shard_map.57 = (s32[8,128]{1,0:T(8,128)}, f32[24,192,128]{2,1,0:T(8,128)}, f32[24,192,128]{2,1,0:T(8,128)}) custom-call(s32[4,2,256]{2,1,0:T(2,128)} %shard_map.55.table_ref, s32[3]{0:T(128)} %pad_add_fusion.place_ref, s32[8,128]{1,0:T(8,128)} %get-tuple-element.58.order_ref, bf16[8,192,128]{2,1,0:T(8,128)(2,1)} %bitcast.49, ...), custom_call_target="tpu_custom_call" | custom-call | flops 1 | bytes 1 | tf_op jit(solution)/shard_map/pallas_call | solution.py:415
  123.5 0.9 copy-done.4
  124.5 1.9 collective-permute-start.6
  126.4 22.6 %shard_map.58 = (s32[8,128]{1,0:T(8,128)}, f32[24,192,128]{2,1,0:T(8,128)}, f32[24,192,128]{2,1,0:T(8,128)}) custom-call(s32[4,2,256]{2,1,0:T(2,128)} %shard_map.55.table_ref, s32[3]{0:T(128)} %pad_add_fusion.place_ref, s32[8,128]{1,0:T(8,128)} %get-tuple-element.65.order_ref, bf16[8,192,128]{2,1,0:T(8,128)(2,1)} %bitcast.50, ...), custom_call_target="tpu_custom_call" | custom-call | flops 1 | bytes 1 | tf_op jit(solution)/shard_map/pallas_call | solution.py:415
  149.0 0.7 copy-done.2
  149.8 14.8 %shard_map.59 = (s32[8,128]{1,0:T(8,128)}, f32[8,192,128]{2,1,0:T(8,128)}, f32[8,192,128]{2,1,0:T(8,128)}) custom-call(s32[4,2,256]{2,1,0:T(2,128)} %shard_map.55.table_ref, s32[3]{0:T(128)} %pad_add_fusion.place_ref, s32[8,128]{1,0:T(8,128)} %get-tuple-element.70.order_ref, bf16[8,192,128]{2,1,0:T(8,128)(2,1)} %copy-done.2, ...), custom_call_target="tpu_custom_call" | custom-call | flops 1 | bytes 1 | tf_op jit(solution)/shard_map/pallas_call | solution.py:415
  164.6 123.8 %shard_map.60 = (s32[8,128]{1,0:T(8,128)}, bf16[8,192,128]{2,1,0:T(8,128)(2,1)}, bf16[8,192,128]{2,1,0:T(8,128)(2,1)}) custom-call(s32[4,2,256]{2,1,0:T(2,128)} %shard_map.55.table_ref, s32[3]{0:T(128)} %pad_add_fusion.place_ref, s32[8,128]{1,0:T(8,128)} %get-tuple-element.72.order_ref, bf16[8,192,128]{2,1,0:T(8,128)(2,1)} %get-tuple-element.106.refs_1_.refs_0_, ...), custom_call_target="tpu_custom_call" | custom-call | flops 1 | bytes 1 | tf_op jit(solution)/shard_map/pallas_call | solution.py:415
  288.5 1.6 collective-permute-start.7
  290.1 1.9 collective-permute-start.8
  292.0 71.0 %shard_map.61 = (s32[8,128]{1,0:T(8,128)}, bf16[8,192,128]{2,1,0:T(8,128)(2,1)}) custom-call(s32[4,2,256]{2,1,0:T(2,128)} %shard_map.55.table_ref, s32[3]{0:T(128)} %pad_add_fusion.place_ref, s32[8,128]{1,0:T(8,128)} %get-tuple-element.79.order_ref, bf16[8,192,128]{2,1,0:T(8,128)(2,1)} %copy-done.2, bf16[4,2,8,192,128]{4,3,2,1,0:T(8,128)(2,1)} %bitcast.34, ...), custom_call_target="tpu_custom_call" | custom-call | flops 1 | bytes 1 | tf_op jit(solution)/shard_map/pallas_call | solution.py:415
  363.0 0.6 collective-permute-start.9
  363.6 0.8 collective-permute-start.10
  364.5 64.7 %shard_map.62 = (s32[8,128]{1,0:T(8,128)}, bf16[8,192,128]{2,1,0:T(8,128)(2,1)}) custom-call(s32[4,2,256]{2,1,0:T(2,128)} %shard_map.55.table_ref, s32[3]{0:T(128)} %pad_add_fusion.place_ref, s32[8,128]{1,0:T(8,128)} %get-tuple-element.86.order_ref, bf16[8,192,128]{2,1,0:T(8,128)(2,1)} %bitcast.51, bf16[4,2,8,192,128]{4,3,2,1,0:T(8,128)(2,1)} %bitcast.35, ...), custom_call_target="tpu_custom_call" | custom-call | flops 1 | bytes 1 | tf_op jit(solution)/shard_map/pallas_call | solution.py:415
  429.2 1.5 collective-permute-start.12
  430.7 0.6 collective-permute-start.11
  431.3 1.5 collective-permute-start.13
  432.8 8.5 %collective-permute-done.12.refs_5_ = bf16[1536,128]{1,0:T(8,128)(2,1)S(1)} collective-permute-done((bf16[1536,128]{1,0:T(8,128)(2,1)S(1)}, bf16[1536,128]{1,0:T(8,128)(2,1)S(1)}, u32[]{:S(2)}, u32[]{:S(2)}) %collective-permute-start.12) | collective-permute-done | bytes 393248 | tf_op jit(solution)/shard_map/ppermute | solution.py:561
  441.3 8.4 %collective-permute-done.11.refs_4_ = bf16[1536,128]{1,0:T(8,128)(2,1)S(1)} collective-permute-done((bf16[1536,128]{1,0:T(8,128)(2,1)}, bf16[1536,128]{1,0:T(8,128)(2,1)S(1)}, u32[]{:S(2)}, u32[]{:S(2)}) %collective-permute-start.11) | collective-permute-done | bytes 393248 | tf_op jit(solution)/shard_map/ppermute | solution.py:561
  449.7 4.6 collective-permute-done.13.refs_6_
  454.4 0.7 copy-done.12
  455.1 5.7 %shard_map.63 = bf16[1536,512]{1,0:T(8,128)(2,1)} custom-call(s32[3]{0:T(128)} %pad_add_fusion.place_ref, bf16[512,1024]{1,0:T(8,128)(2,1)} %near_ref.1, bf16[512,512]{1,0:T(8,128)(2,1)} %copy-done.5, bf16[1536,128]{1,0:T(8,128)(2,1)} %bitcast.61, bf16[1536,128]{1,0:T(8,128)(2,1)} %copy-done.7, bf16[1536,128]{1,0:T(8,128)(2,1)} %copy-done.9, ...), custom_call_target="tpu_custom_call" | custom-call | flops 1610612736 | bytes 6291456 | tf_op jit(solution)/shard_map/pallas_call | solution.py:459
  (43 shorter events, 0.2 us)
Async XLA Ops:
  6.5 72.7 %all-gather.9.cloned.1.call-start = ((), (), s32[]{:S(2)}) async-start(), calls=%async_computation | async-start | bytes 3932160 | tf_op jit(solution)/shard_map/all_gather | solution.py:558
  10.4 90.7 %all-gather.11.cloned.1.call-start = ((), (), s32[]{:S(2)}) async-start(), calls=%async_computation.1 | async-start | bytes 3932160 | tf_op jit(solution)/shard_map/all_gather | solution.py:558
  11.5 8.9 %copy-start.14 = (s32[1024,2]{0,1:T(2,128)S(1)}, s32[1024,2]{0,1:T(2,128)}, u32[]{:S(2)}) copy-start(s32[1024,2]{0,1:T(2,128)} %param.8) | copy-start | bytes 24580
  11.5 53.7 %copy-start.1 = (bf16[512,1024]{1,0:T(8,128)(2,1)S(1)}, bf16[512,1024]{1,0:T(8,128)(2,1)}, u32[]{:S(2)}) copy-start(bf16[512,1024]{1,0:T(8,128)(2,1)} %near_ref.1) | copy-start | bytes 3145732
  11.5 21.3 %collective-permute-start = (bf16[2,8,192,128]{3,2,1,0:T(8,128)(2,1)}, bf16[2,8,192,128]{3,2,1,0:T(8,128)(2,1)S(1)}, u32[]{:S(2)}, u32[]{:S(2)}) collective-permute-start(bf16[2,8,192,128]{3,2,1,0:T(8,128)(2,1)} %pad_maximum_fusion), channel_id=1, source_target_pairs={{0,8},{2,10},{4,12},{6,14},{8,0},{10,2},{12,4},{14,6},{16,24},{18,... | collective-permute-start | bytes 2359304 | tf_op jit(solution)/shard_map/ppermute | solution.py:552
  17.9 33.6 %collective-permute-start.1 = (bf16[2,8,192,128]{3,2,1,0:T(8,128)(2,1)}, bf16[2,8,192,128]{3,2,1,0:T(8,128)(2,1)}, u32[]{:S(2)}, u32[]{:S(2)}) collective-permute-start(bf16[2,8,192,128]{3,2,1,0:T(8,128)(2,1)} %pad_maximum_fusion.1), channel_id=1, source_target_pairs={{0,24},{2,26},{4,28},{6,30},{8,16},{10,18},{12,20},{14,22},{16,8},... | collective-permute-start | bytes 2359304 | tf_op jit(solution)/shard_map/ppermute | solution.py:552
  32.8 18.7 %copy-start.3 = (bf16[2,8,192,128]{3,2,1,0:T(8,128)(2,1)}, bf16[2,8,192,128]{3,2,1,0:T(8,128)(2,1)S(1)}, u32[]{:S(2)}) copy-start(bf16[2,8,192,128]{3,2,1,0:T(8,128)(2,1)S(1)} %collective-permute-done) | copy-start | bytes 2359300
  51.6 74.9 %all-gather.13.cloned.1.call-start = ((), (), s32[]{:S(2)}) async-start(), calls=%async_computation.2 | async-start | bytes 3932160 | tf_op jit(solution)/shard_map/all_gather | solution.py:558
  51.6 14.3 %collective-permute-start.2 = (bf16[8,192,128]{2,1,0:T(8,128)(2,1)}, bf16[8,192,128]{2,1,0:T(8,128)(2,1)}, u32[]{:S(2)}, u32[]{:S(2)}) collective-permute-start(bf16[8,192,128]{2,1,0:T(8,128)(2,1)} %bitcast.7), channel_id=1, source_target_pairs={{0,24},{2,26},{4,28},{6,30},{8,16},{10,18},{12,20},{14,22},{16,8},... | collective-permute-start | bytes 1179656 | tf_op jit(solution)/shard_map/ppermute | solution.py:552
  54.0 18.1 %collective-permute-start.3 = (bf16[8,192,128]{2,1,0:T(8,128)(2,1)}, bf16[8,192,128]{2,1,0:T(8,128)(2,1)S(1)}, u32[]{:S(2)}, u32[]{:S(2)}) collective-permute-start(bf16[8,192,128]{2,1,0:T(8,128)(2,1)} %bitcast.8), channel_id=1, source_target_pairs={{0,8},{2,10},{4,12},{6,14},{8,0},{10,2},{12,4},{14,6},{16,24},{18,... | collective-permute-start | bytes 1179656 | tf_op jit(solution)/shard_map/ppermute | solution.py:552
  72.0 7.8 %copy-start = (bf16[8,192,128]{2,1,0:T(8,128)(2,1)}, bf16[8,192,128]{2,1,0:T(8,128)(2,1)S(1)}, u32[]{:S(2)}) copy-start(bf16[8,192,128]{2,1,0:T(8,128)(2,1)S(1)} %collective-permute-done.3.refs_2_.refs_1_) | copy-start | bytes 1179652
  76.1 88.5 %all-gather.15.cloned.1.call-start = ((), (), s32[]{:S(2)}) async-start(), calls=%async_computation.3 | async-start | bytes 3932160 | tf_op jit(solution)/shard_map/all_gather | solution.py:558
  76.1 47.4 %collective-permute-start.4 = (bf16[2,8,192,128]{3,2,1,0:T(8,128)(2,1)S(1)}, bf16[2,8,192,128]{3,2,1,0:T(8,128)(2,1)S(1)}, u32[]{:S(2)}, u32[]{:S(2)}) collective-permute-start(bf16[2,8,192,128]{3,2,1,0:T(8,128)(2,1)S(1)} %pad_maximum_fusion.2), channel_id=1, source_target_pairs={{0,16},{2,18},{4,20},{6,22},{8,24},{10,26},{12,28},{14,30},{16,0},... | collective-permute-start | bytes 2359304 | tf_op jit(solution)/shard_map/ppermute | solution.py:552
  77.8 45.7 %collective-permute-start.5 = (bf16[512,512]{1,0:T(8,128)(2,1)S(1)}, bf16[512,512]{1,0:T(8,128)(2,1)S(1)}, u32[]{:S(2)}, u32[]{:S(2)}) collective-permute-start(bf16[512,512]{1,0:T(8,128)(2,1)S(1)} %constant_dynamic-slice_fusion.4), channel_id=1, source_target_pairs={{0,1},{1,0},{2,3},{3,2},{4,5},{5,4},{6,7},{7,6},{8,9},{9,8},{10,11... | collective-permute-start | bytes 1572872 | tf_op jit(solution)/shard_map/ppermute | solution.py:561
  101.1 23.3 %copy-start.13 = (bf16[1536,128]{1,0:T(8,128)(2,1)S(1)}, bf16[1536,128]{1,0:T(8,128)(2,1)}, u32[]{:S(2)}) copy-start(bf16[1536,128]{1,0:T(8,128)(2,1)} %get-tuple-element.104) | copy-start | bytes 1179652
  123.5 41.1 %copy-start.5 = (bf16[512,512]{1,0:T(8,128)(2,1)}, bf16[512,512]{1,0:T(8,128)(2,1)S(1)}, u32[]{:S(2)}) copy-start(bf16[512,512]{1,0:T(8,128)(2,1)S(1)} %collective-permute-done.5.far_ref) | copy-start | bytes 1572868
  123.5 0.9 copy-start.4
  124.5 24.6 %collective-permute-start.6 = (bf16[8,192,128]{2,1,0:T(8,128)(2,1)S(1)}, bf16[8,192,128]{2,1,0:T(8,128)(2,1)S(1)}, u32[]{:S(2)}, u32[]{:S(2)}) collective-permute-start(bf16[8,192,128]{2,1,0:T(8,128)(2,1)S(1)} %bitcast.62), channel_id=1, source_target_pairs={{0,16},{2,18},{4,20},{6,22},{8,24},{10,26},{12,28},{14,30},{16,0},... | collective-permute-start | bytes 1179656 | tf_op jit(solution)/shard_map/ppermute | solution.py:552
  149.0 0.8 copy-start.2
  288.5 74.5 %collective-permute-start.7 = (bf16[1536,128]{1,0:T(8,128)(2,1)}, bf16[1536,128]{1,0:T(8,128)(2,1)S(1)}, u32[]{:S(2)}, u32[]{:S(2)}) collective-permute-start(bf16[1536,128]{1,0:T(8,128)(2,1)} %bitcast.67), channel_id=1, source_target_pairs={{0,24},{2,26},{4,28},{6,30},{8,16},{10,18},{12,20},{14,22},{16,8},... | collective-permute-start | bytes 1179656 | tf_op jit(solution)/shard_map/ppermute | solution.py:552
  290.1 72.9 %collective-permute-start.8 = (bf16[1536,128]{1,0:T(8,128)(2,1)}, bf16[1536,128]{1,0:T(8,128)(2,1)S(1)}, u32[]{:S(2)}, u32[]{:S(2)}) collective-permute-start(bf16[1536,128]{1,0:T(8,128)(2,1)} %bitcast.66), channel_id=1, source_target_pairs={{0,8},{2,10},{4,12},{6,14},{8,0},{10,2},{12,4},{14,6},{16,24},{18,... | collective-permute-start | bytes 1179656 | tf_op jit(solution)/shard_map/ppermute | solution.py:552
  363.0 66.2 %copy-start.6 = (bf16[1536,128]{1,0:T(8,128)(2,1)}, bf16[1536,128]{1,0:T(8,128)(2,1)S(1)}, u32[]{:S(2)}) copy-start(bf16[1536,128]{1,0:T(8,128)(2,1)S(1)} %collective-permute-done.7.refs_3_) | copy-start | bytes 1179652
  363.0 66.2 %copy-start.7 = (bf16[1536,128]{1,0:T(8,128)(2,1)}, bf16[1536,128]{1,0:T(8,128)(2,1)S(1)}, u32[]{:S(2)}) copy-start(bf16[1536,128]{1,0:T(8,128)(2,1)S(1)} %collective-permute-done.8.refs_1_) | copy-start | bytes 1179652
  363.0 67.7 %collective-permute-start.9 = (bf16[1536,128]{1,0:T(8,128)(2,1)S(1)}, bf16[1536,128]{1,0:T(8,128)(2,1)S(1)}, u32[]{:S(2)}, u32[]{:S(2)}) collective-permute-start(bf16[1536,128]{1,0:T(8,128)(2,1)S(1)} %collective-permute-done.7.refs_3_), channel_id=1, source_target_pairs={{0,1},{1,0},{2,3},{3,2},{4,5},{5,4},{6,7},{7,6},{8,9},{9,8},{10,11... | collective-permute-start | bytes 1179656 | tf_op jit(solution)/shard_map/ppermute | solution.py:561
  363.6 67.7 %collective-permute-start.10 = (bf16[1536,128]{1,0:T(8,128)(2,1)}, bf16[1536,128]{1,0:T(8,128)(2,1)S(1)}, u32[]{:S(2)}, u32[]{:S(2)}) collective-permute-start(bf16[1536,128]{1,0:T(8,128)(2,1)} %bitcast.65), channel_id=1, source_target_pairs={{0,16},{2,18},{4,20},{6,22},{8,24},{10,26},{12,28},{14,30},{16,0},... | collective-permute-start | bytes 1179656 | tf_op jit(solution)/shard_map/ppermute | solution.py:552
  429.2 12.1 %collective-permute-start.12 = (bf16[1536,128]{1,0:T(8,128)(2,1)S(1)}, bf16[1536,128]{1,0:T(8,128)(2,1)S(1)}, u32[]{:S(2)}, u32[]{:S(2)}) collective-permute-start(bf16[1536,128]{1,0:T(8,128)(2,1)S(1)} %collective-permute-done.8.refs_1_), channel_id=1, source_target_pairs={{0,1},{1,0},{2,3},{3,2},{4,5},{5,4},{6,7},{7,6},{8,9},{9,8},{10,11... | collective-permute-start | bytes 1179656 | tf_op jit(solution)/shard_map/ppermute | solution.py:561
  430.7 23.6 %copy-start.8 = (bf16[1536,128]{1,0:T(8,128)(2,1)}, bf16[1536,128]{1,0:T(8,128)(2,1)S(1)}, u32[]{:S(2)}) copy-start(bf16[1536,128]{1,0:T(8,128)(2,1)S(1)} %collective-permute-done.9.refs_7_) | copy-start | bytes 1179652
  430.7 19.0 %collective-permute-start.11 = (bf16[1536,128]{1,0:T(8,128)(2,1)}, bf16[1536,128]{1,0:T(8,128)(2,1)S(1)}, u32[]{:S(2)}, u32[]{:S(2)}) collective-permute-start(bf16[1536,128]{1,0:T(8,128)(2,1)} %bitcast.60), channel_id=1, source_target_pairs={{0,1},{1,0},{2,3},{3,2},{4,5},{5,4},{6,7},{7,6},{8,9},{9,8},{10,11... | collective-permute-start | bytes 1179656 | tf_op jit(solution)/shard_map/ppermute | solution.py:561
  431.3 23.1 %copy-start.9 = (bf16[1536,128]{1,0:T(8,128)(2,1)}, bf16[1536,128]{1,0:T(8,128)(2,1)S(1)}, u32[]{:S(2)}) copy-start(bf16[1536,128]{1,0:T(8,128)(2,1)S(1)} %collective-permute-done.10.refs_2_) | copy-start | bytes 1179652
  431.3 23.1 %collective-permute-start.13 = (bf16[1536,128]{1,0:T(8,128)(2,1)S(1)}, bf16[1536,128]{1,0:T(8,128)(2,1)S(1)}, u32[]{:S(2)}, u32[]{:S(2)}) collective-permute-start(bf16[1536,128]{1,0:T(8,128)(2,1)S(1)} %collective-permute-done.10.refs_2_), channel_id=1, source_target_pairs={{0,1},{1,0},{2,3},{3,2},{4,5},{5,4},{6,7},{7,6},{8,9},{9,8},{10,11... | collective-permute-start | bytes 1179656 | tf_op jit(solution)/shard_map/ppermute | solution.py:561
  441.3 13.1 %copy-start.10 = (bf16[1536,128]{1,0:T(8,128)(2,1)}, bf16[1536,128]{1,0:T(8,128)(2,1)S(1)}, u32[]{:S(2)}) copy-start(bf16[1536,128]{1,0:T(8,128)(2,1)S(1)} %collective-permute-done.12.refs_5_) | copy-start | bytes 1179652
  449.7 4.6 copy-start.11
  454.4 0.8 copy-start.12
Sparse Core Ops, SparseCore 0:
  10.6 31.2 all-gather.8
  51.7 39.1 all-gather.10
  92.4 28.5 all-gather.12
  124.6 27.9 all-gather.14

commit v3 on v1

--- a/solution.py
+++ b/solution.py
@@ -156,7 +156,7 @@
     out_refs, refs = refs[:outs], refs[outs:]
     sum_ref, total_ref, pair_ref, wide_ref, query_ref, score_ref, arrived, left = refs[:8]
     frames_here = query_refs[0].shape[0]
-    group = pair_ref.shape[1]
+    group = pair_ref.shape[2]
     per_source = max(pair_refs[0][0].shape[0] // group, 1)
     first_frame = chunks[0] * frames_here
     query_frames = len(chunks) * frames_here
@@ -164,14 +164,13 @@
 
     def copies(block, slot, source):
         refs_here = pair_refs[source]
-        if len(refs_here) == 1:
-            part = refs_here[0].at[pl.ds(block % per_source * group, group)]
-            return [pltpu.make_async_copy(part, pair_ref.at[slot], arrived.at[slot])]
-        result = []
-        for far, ref in enumerate(refs_here):
-            here = pair_ref.at[slot, pl.ds((place_ref[1] // 2 ^ far) * 2, 2)]
-            result.append(pltpu.make_async_copy(ref, here, arrived.at[slot]))
-        return result
+        devices = pl.ds(block % per_source * group, group)
+        return [
+            pltpu.make_async_copy(
+                refs_here[0].at[devices, kind], pair_ref.at[slot, kind], arrived.at[2 * slot + kind]
+            )
+            for kind in range(2)
+        ]
 
     def fetch(block, slot):
         for source in range(len(sources)):
@@ -189,8 +188,11 @@
             def _():
                 fetch(block + 1, (turn + 1) % 2)
 
-            whole = pair_ref.at[turn % 2]
-            pltpu.make_async_copy(whole, whole, arrived.at[turn % 2]).wait()
+            def wait_for(kind):
+                here = pair_ref.at[turn % 2, kind]
+                pltpu.make_async_copy(here, here, arrived.at[2 * (turn % 2) + kind]).wait()
+
+            wait_for(0)
 
             def units_of(index):
                 first = index * 2 * UNROLL
@@ -207,6 +209,8 @@
                 begins = table_ref[block, 1, chunk]
                 if ahead:
                     ahead(turn % 2, units_of(begins))
+                if index == 0:
+                    wait_for(1)
                 lax.fori_loop(begins, table_ref[block, 1, chunk + 1], several, 0)
                 if behind:
                     behind(index)
@@ -227,7 +231,7 @@
 
     def scores_of(slot, unit):
         query_frame, keys = frames_at(slot, unit)
-        held = jnp.concatenate([pair_ref[slot, device, 0, frame] for slot, device, frame in keys], axis=0)
+        held = jnp.concatenate([pair_ref[slot, 0, device, frame] for slot, device, frame in keys], axis=0)
         return lax.dot_general(
             wide_ref[query_frame], held, (((1,), (1,)), ((), ())), preferred_element_type=jnp.float32
         )
@@ -238,7 +242,7 @@
         return jnp.where(lane < TOKF, bias[0], bias[1])
 
     def sums_of(keys, weights):
-        held = jnp.concatenate([pair_ref[slot, device, 1, frame] for slot, device, frame in keys], axis=0)
+        held = jnp.concatenate([pair_ref[slot, 1, device, frame] for slot, device, frame in keys], axis=0)
         return by_head(
             jnp.dot(weights.astype(jnp.bfloat16), held, preferred_element_type=jnp.float32)
         )
@@ -287,7 +291,7 @@
             taken.append(
                 [
                     pltpu.make_async_copy(
-                        old_ref.at[source], new_ref.at[frames_of[place]], arrived.at[2 + place]
+                        old_ref.at[source], new_ref.at[frames_of[place]], arrived.at[4 + place]
                     )
                     for old_ref, new_ref in zip(old_refs, (sum_ref, total_ref))
                 ]
@@ -323,7 +327,7 @@
         if states:
             for ref in (sum_ref, total_ref):
                 part = ref.at[frames_of[index]]
-                pltpu.make_async_copy(part, part, arrived.at[2 + index]).wait()
+                pltpu.make_async_copy(part, part, arrived.at[4 + index]).wait()
 
     def leave(index):
         if not ends:
@@ -404,11 +408,11 @@
     room = pltpu.VMEM(shape, jnp.float32)
     wide = (shape[0], PACKED, LANES)
     common = [
-        pltpu.VMEM((2, group) + pairs[0][0].shape[1:], queries[0].dtype),
+        pltpu.VMEM((2, 2, group) + pairs[0][0].shape[2:], queries[0].dtype),
         pltpu.VMEM(wide, queries[0].dtype),
         pltpu.VMEM((len(chunks),) + queries[0].shape, queries[0].dtype),
         pltpu.VMEM((UNROLL, PACKED, PACKED), jnp.float32),
-        pltpu.SemaphoreType.DMA((2 + len(chunks),)),
+        pltpu.SemaphoreType.DMA((4 + len(chunks),)),
         pltpu.SemaphoreType.DMA((len(chunks),)),
     ]
     listed = [array for plane in pairs for array in plane] + [array for pair in state for array in pair]
@@ -438,37 +442,51 @@
     )(table, places, order, *queries, *listed)
 
 
-def project_kernel(parts, place_ref, near_ref, far_ref, *refs):
-    plane, side = place_ref[0], place_ref[2]
-    out_ref = refs[2 * parts]
-    columns = out_ref.shape[1]
-    mine = pl.ds(pl.multiple_of(side * columns, columns), columns)
-    rows = [pl.ds(pl.multiple_of((plane ^ part) * LANES, LANES), LANES) for part in range(parts)]
-    merged = jnp.concatenate([ref[...] for ref in refs[: 2 * parts]], axis=1)
-    weight = [near_ref[row, mine] for row in rows] + [far_ref[row, :] for row in rows]
-    out_ref[...] = jnp.dot(
-        merged, jnp.concatenate(weight, axis=0), preferred_element_type=jnp.float32
-    ).astype(out_ref.dtype)
-
-
-def project(merged, others, near, far, places):
-    rows = merged[0].shape[0]
+def project_kernel(parts, place_ref, *refs):
+    del place_ref
+    row_refs, weight_refs, refs = refs[:parts], refs[parts : 2 * parts], refs[2 * parts :]
+    out_ref = refs[-1]
+    total = jnp.dot(
+        jnp.concatenate([ref[...] for ref in row_refs], axis=1),
+        jnp.concatenate([ref[...] for ref in weight_refs], axis=0),
+        preferred_element_type=jnp.float32,
+    )
+    if len(refs) > 1:
+        total = total + refs[0][...]
+    out_ref[...] = total.astype(out_ref.dtype)
+
+
+def project(parts, near, far, places, total, ends):
+    rows = parts[0][2].shape[0]
     tile = rows // 4 if rows % 64 == 0 else rows
-    parts = merged + others
     columns = far.shape[1]
+
+    def weight_spec(other, distance):
+        def place(row, at):
+            return (at[0] ^ distance, 0 if other else at[2])
+
+        return pl.BlockSpec((LANES, columns), place)
+
+    kept = pl.BlockSpec((tile, columns), lambda row, at: (row, 0))
     return pl.pallas_call(
-        functools.partial(project_kernel, len(merged)),
-        grid=(rows // tile,),
-        in_specs=[pl.BlockSpec(memory_space=pltpu.SMEM)]
-        + [pl.BlockSpec(weight.shape, lambda row: (0, 0)) for weight in (near, far)]
-        + [pl.BlockSpec((tile, part.shape[1]), lambda row: (row, 0)) for part in parts],
-        out_specs=pl.BlockSpec((tile, columns), lambda row: (row, 0)),
-        out_shape=jax.ShapeDtypeStruct((rows, columns), parts[0].dtype),
+        functools.partial(project_kernel, len(parts)),
+        grid_spec=pltpu.PrefetchScalarGridSpec(
+            num_scalar_prefetch=1,
+            grid=(rows // tile,),
+            in_specs=[pl.BlockSpec((tile, LANES), lambda row, at: (row, 0)) for _ in parts]
+            + [weight_spec(other, distance) for other, distance, _ in parts]
+            + ([] if total is None else [kept]),
+            out_specs=kept,
+        ),
+        out_shape=jax.ShapeDtypeStruct((rows, columns), near.dtype if ends else jnp.float32),
         compiler_params=pltpu.CompilerParams(vmem_limit_bytes=VMEM_LIMIT),
-        cost_estimate=pl.CostEstimate(
-            flops=4 * rows * far.size, bytes_accessed=rows * 4096, transcendentals=0
-        ),
-    )(places, near, far, *parts)
+        cost_estimate=pl.CostEstimate(flops=1, bytes_accessed=1, transcendentals=0),
+    )(
+        places,
+        *(part for _, _, part in parts),
+        *(far if other else near for other, _, _ in parts),
+        *(() if total is None else (total,)),
+    )
 
 
 def spread(queries, pairs, far, table, places, swap, across, gather, plane_size):
@@ -495,19 +513,19 @@
         return [gather(pairs[distance], plane_size)]
 
     keyed = [gathered(0), None, None, None]
-    queries[3], queries[1] = swap(queries[3], 3), swap(queries[1], 1)
-    queries[3], queries[1], pairs[1], table, order = barrier(
-        (queries[3], queries[1], pairs[1], table, order)
-    )
-    pairs[1] = swap(pairs[1], 1)
-    pairs[1], pairs[3], far, order = barrier((pairs[1], pairs[3], far, order))
+    pairs[1], queries[3] = swap(pairs[1], 1), swap(queries[3], 3)
+    pairs[1], queries[3], queries[1], pairs[3], table, far, order = barrier(
+        (pairs[1], queries[3], queries[1], pairs[3], table, far, order)
+    )
     keyed[1] = gathered(1)
-    pairs[3], far = swap(pairs[3], 3), across(far)
-    order, *state = run([0, 3, 1], 0, keyed, [])
-    pairs[3], pairs[2], far, order = barrier((pairs[3], pairs[2], far, order))
+    pairs[3], queries[1], far = swap(pairs[3], 3), swap(queries[1], 1), across(far)
+    order, *early = run([0, 3], 0, keyed, [])
+    queries[1], far, order = barrier((queries[1], far, order))
+    order, *late = run([1], 0, keyed, [])
+    pairs[3], pairs[2], order = barrier((pairs[3], pairs[2], order))
     keyed[3] = gathered(3)
     pairs[2] = swap(pairs[2], 2)
-    order, *state = run([0, 3, 1], 1, keyed, [state])
+    order, *state = run([0, 3, 1], 1, keyed, [early, late])
     pairs[2], queries[2], order = barrier((pairs[2], queries[2], order))
     keyed[2] = gathered(2)
     queries[2] = swap(queries[2], 2)
@@ -519,16 +537,15 @@
     def rows_of(out):
         return out.reshape(-1, LANES)
 
+    order, *outs = run([0, 3, 1], 2, keyed, [state], True)
+    merged[0], out, near_out, order = barrier(tuple(map(rows_of, outs)) + (order,))
+    merged[3], merged[1], others[0] = swap(out, 3), swap(near_out, 1), across(merged[0])
     order, out = run([2], 2, keyed, [last], True, 2)
-    out, order = barrier((rows_of(out), order))
-    merged[2] = swap(out, 2)
-    order, near_out, out = run([0, 3], 2, keyed, [state], True)
-    merged[0], out, merged[2], order = barrier((rows_of(near_out), rows_of(out), merged[2], order))
-    merged[3], others[0], others[2] = swap(out, 3), across(merged[0]), across(merged[2])
-    order, out = run([1], 2, keyed, [state], True)
-    out, merged[3], others[0], others[2] = barrier((rows_of(out), merged[3], others[0], others[2]))
-    merged[1], others[3] = swap(out, 1), across(merged[3])
-    others[1] = across(merged[1])
+    out, merged[3], merged[1], others[0] = barrier(
+        (rows_of(out), merged[3], merged[1], others[0])
+    )
+    merged[2], others[1], others[3] = swap(out, 2), across(merged[1]), across(merged[3])
+    others[2] = across(merged[2])
     return merged, others, far
 
 
@@ -583,12 +600,16 @@
             return lax.psum_scatter(
                 term.astype(out.dtype), "heads", scatter_dimension=1, tiled=True
             )
-        return project([out], [across(out)], out_weight, across(far), places)
+        parts = [(False, 0, out), (True, 0, across(out))]
+        return project(parts, out_weight, across(far), places, None, True)
     assert two
     merged, others, far = spread(
         queries, pairs, far, table, places, swap, across, gather, plane_size
     )
-    return project(merged, others, out_weight, far, places)
+    ready = [(False, distance, merged[distance]) for distance in range(planes)]
+    ready += [(True, distance, others[distance]) for distance in (0, 1, 3)]
+    total = project(ready, out_weight, far, places, None, False)
+    return project([(True, 2, others[2])], out_weight, far, places, total, True)
 
 
 def solution(mesh):

time: 460 us -> 460 us (level)
  starting transfers between devices: 32.2 us -> 23.3 us
  Pallas kernels: 350 us -> 358 us
    ppermute x9, starting transfers between devices: 25.6 us -> 16.6 us  [swap(): lax.ppermute(array, 'frames', [(index, index ^ distance * axis) for index...]
    ppermute x9, waiting for transfers between devices: 40.6 us -> 49.3 us  [swap(): lax.ppermute(array, 'frames', [(index, index ^ distance * axis) for index...]
    ppermute x5, waiting for transfers between devices: 7.42 us -> 0.58 us  [across(): return lax.ppermute(array, 'heads', [(0, 1), (1, 0)])]
    pallas_call x1 -> x2, Pallas kernels: 5.74 us -> 11.5 us  [project(): pl.pallas_call(functools.partial(project_kernel, len(parts)), grid_spec=p...]
  transfers between devices with their start and end apart: 18 -> 18, of which waited for: 6 -> 5; matrix products, arithmetic and copies ran while one was open for 1% -> 1% of each run, Pallas kernels for 60% -> 36%
where the time goes in v3:
time: 460 us; the launch traced here: 461 us
  Pallas kernels  358 us (78%)
  waiting for transfers between devices  50 us (11%)
  starting transfers between devices  23.3 us (5%)
  between operations  13.4 us (3%)
  local copies, waits for them, and re-layouts  11.6 us (3%)
    pallas_call x7, Pallas kernels, attend(): pl.pallas_call(functools.partial(attend_kernel, begin, number, tuple(chun...  341 us
    ppermute x9, waiting for transfers between devices, swap(): lax.ppermute(array, 'frames', [(index, index ^ distance * axis) for index...  49.3 us
    ppermute x9, starting transfers between devices, swap(): lax.ppermute(array, 'frames', [(index, index ^ distance * axis) for index...  16.6 us
    pallas_call x2, Pallas kernels, project(): pl.pallas_call(functools.partial(project_kernel, len(parts)), grid_spec=p...  11.5 us
  transfers between devices with their start and end apart: 18, of which 5 were waited for; matrix products, arithmetic and copies ran while one was open for 1% of the time, Pallas kernels for 36%

profile of v3, /device:TPU:0, one launch (start us, length us, event | category | flops | bytes accessed | tf_op | source)
XLA Modules:
  0.0 461.3 jit_solution(14883822130057617128)
XLA Ops:
  6.5 1.6 constant_dynamic-slice_fusion.2
  8.2 0.3 copy-done.4
  8.5 0.5 copy-done.5
  8.9 1.6 constant_dynamic-slice_fusion
  10.5 0.9 pad_maximum_fusion.3
  11.5 0.0 all-gather.11.cloned.1.call-start
  11.6 1.0 pad_maximum_fusion
  12.5 3.0 collective-permute-start
  15.5 2.5 collective-permute-start.1
  18.0 0.6 copy.8
  18.6 0.6 pad_add_fusion.place_ref
  19.2 5.6 %shard_map.55.table_ref = s32[4,2,256]{2,1,0:T(2,128)} custom-call(s32[3]{0:T(128)} %pad_add_fusion.place_ref, s32[2,8,128]{2,1,0:T(8,128)} %bitcast.59), custom_call_target="tpu_custom_call" | custom-call | tf_op jit(solution)/shard_map/pallas_call | solution.py:130
  24.8 0.9 constant_dynamic-slice_fusion.6
  25.7 0.9 pad_maximum_fusion.1
  26.6 17.4 %collective-permute-done.1.refs_1_ = bf16[8,192,128]{2,1,0:T(8,128)(2,1)S(1)} collective-permute-done((bf16[8,192,128]{2,1,0:T(8,128)(2,1)}, bf16[8,192,128]{2,1,0:T(8,128)(2,1)S(1)}, u32[]{:S(2)}, u32[]{:S(2)}) %collective-permute-start.1) | collective-permute-done | bytes 393248 | tf_op jit(solution)/shard_map/ppermute | solution.py:569
  44.1 1.6 collective-permute-start.2
  45.7 1.5 collective-permute-start.4
  47.3 1.0 pad_maximum_fusion.2
  48.3 0.6 broadcast_in_dim.3.order_ref
  48.9 16.1 %shard_map.56 = (s32[8,128]{1,0:T(8,128)}, f32[16,192,128]{2,1,0:T(8,128)}, f32[16,192,128]{2,1,0:T(8,128)}) custom-call(s32[4,2,256]{2,1,0:T(2,128)} %shard_map.55.table_ref, s32[3]{0:T(128)} %pad_add_fusion.place_ref, s32[8,128]{1,0:T(8,128)} %broadcast_in_dim.3.order_ref, bf16[8,192,128]{2,1,0:T(8,128)(2,1)} %bitcast.42, bf16[8,192,128]{2,1,0:T(8,128)(2,1)} %copy-done.2, ...), custom_call_target="tpu_custom_call" | custom-call | flops 1 | bytes 1 | tf_op jit(solution)/shard_map/pallas_call | solution.py:419
  65.0 8.0 %collective-permute-done.3.refs_0_.refs_2_ = bf16[8,192,128]{2,1,0:T(8,128)(2,1)S(1)} collective-permute-done((bf16[8,192,128]{2,1,0:T(8,128)(2,1)S(1)}, bf16[8,192,128]{2,1,0:T(8,128)(2,1)S(1)}, u32[]{:S(2)}, u32[]{:S(2)}) %collective-permute-start.3) | collective-permute-done | bytes 393248 | tf_op jit(solution)/shard_map/ppermute | solution.py:569
  73.1 0.8 copy-done.3
  73.8 9.3 %shard_map.57 = (s32[8,128]{1,0:T(8,128)}, f32[8,192,128]{2,1,0:T(8,128)}, f32[8,192,128]{2,1,0:T(8,128)}) custom-call(s32[4,2,256]{2,1,0:T(2,128)} %shard_map.55.table_ref, s32[3]{0:T(128)} %pad_add_fusion.place_ref, s32[8,128]{1,0:T(8,128)} %get-tuple-element.58.order_ref, bf16[8,192,128]{2,1,0:T(8,128)(2,1)} %copy-done.3, ...), custom_call_target="tpu_custom_call" | custom-call | flops 1 | bytes 1 | tf_op jit(solution)/shard_map/pallas_call | solution.py:419
  83.2 0.9 copy-done.7
  84.1 0.6 collective-permute-start.5
  84.8 23.4 %shard_map.58 = (s32[8,128]{1,0:T(8,128)}, f32[24,192,128]{2,1,0:T(8,128)}, f32[24,192,128]{2,1,0:T(8,128)}) custom-call(s32[4,2,256]{2,1,0:T(2,128)} %shard_map.55.table_ref, s32[3]{0:T(128)} %pad_add_fusion.place_ref, s32[8,128]{1,0:T(8,128)} %get-tuple-element.62.order_ref, bf16[8,192,128]{2,1,0:T(8,128)(2,1)} %bitcast.43, ...), custom_call_target="tpu_custom_call" | custom-call | flops 1 | bytes 1 | tf_op jit(solution)/shard_map/pallas_call | solution.py:419
  108.2 12.7 %collective-permute-done.5 = bf16[2,8,192,128]{3,2,1,0:T(8,128)(2,1)S(1)} collective-permute-done((bf16[2,8,192,128]{3,2,1,0:T(8,128)(2,1)S(1)}, bf16[2,8,192,128]{3,2,1,0:T(8,128)(2,1)S(1)}, u32[]{:S(2)}, u32[]{:S(2)}) %collective-permute-start.5) | collective-permute-done | bytes 786464 | tf_op jit(solution)/shard_map/ppermute | solution.py:569
  120.9 0.9 copy-done.9
  121.9 0.1 collective-permute-start.6
  122.0 22.4 %shard_map.59 = (s32[8,128]{1,0:T(8,128)}, f32[24,192,128]{2,1,0:T(8,128)}, f32[24,192,128]{2,1,0:T(8,128)}) custom-call(s32[4,2,256]{2,1,0:T(2,128)} %shard_map.55.table_ref, s32[3]{0:T(128)} %pad_add_fusion.place_ref, s32[8,128]{1,0:T(8,128)} %get-tuple-element.70.order_ref, bf16[8,192,128]{2,1,0:T(8,128)(2,1)} %bitcast.44, ...), custom_call_target="tpu_custom_call" | custom-call | flops 1 | bytes 1 | tf_op jit(solution)/shard_map/pallas_call | solution.py:419
  144.4 0.7 copy-done.6
  145.2 14.6 %shard_map.60 = (s32[8,128]{1,0:T(8,128)}, f32[8,192,128]{2,1,0:T(8,128)}, f32[8,192,128]{2,1,0:T(8,128)}) custom-call(s32[4,2,256]{2,1,0:T(2,128)} %shard_map.55.table_ref, s32[3]{0:T(128)} %pad_add_fusion.place_ref, s32[8,128]{1,0:T(8,128)} %get-tuple-element.75.order_ref, bf16[8,192,128]{2,1,0:T(8,128)(2,1)} %copy-done.6, ...), custom_call_target="tpu_custom_call" | custom-call | flops 1 | bytes 1 | tf_op jit(solution)/shard_map/pallas_call | solution.py:419
  159.8 186.3 %shard_map.61 = (s32[8,128]{1,0:T(8,128)}, bf16[8,192,128]{2,1,0:T(8,128)(2,1)}, bf16[8,192,128]{2,1,0:T(8,128)(2,1)}, bf16[8,192,128]{2,1,0:T(8,128)(2,1)}) custom-call(s32[4,2,256]{2,1,0:T(2,128)} %shard_map.55.table_ref, s32[3]{0:T(128)} %pad_add_fusion.place_ref, s32[8,128]{1,0:T(8,128)} %get-tuple-element.77.order_ref, bf16[8,192,128]{2,1,0:T(8,128)(2,1)} %bitcast.45, ...), custom_call_target="tpu_custom_call" | custom-call | flops 1 | bytes 1 | tf_op jit(solution)/shard_map/pallas_call | solution.py:419
  346.1 0.1 collective-permute-start.7
  346.1 2.3 collective-permute-start.8
  348.4 1.2 collective-permute-start.9
  349.7 69.2 %shard_map.62 = (s32[8,128]{1,0:T(8,128)}, bf16[8,192,128]{2,1,0:T(8,128)(2,1)}) custom-call(s32[4,2,256]{2,1,0:T(2,128)} %shard_map.55.table_ref, s32[3]{0:T(128)} %pad_add_fusion.place_ref, s32[8,128]{1,0:T(8,128)} %get-tuple-element.85.order_ref, bf16[8,192,128]{2,1,0:T(8,128)(2,1)} %copy-done.6, bf16[4,2,8,192,128]{4,3,2,1,0:T(8,128)(2,1)} %bitcast.32, ...), custom_call_target="tpu_custom_call" | custom-call | flops 1 | bytes 1 | tf_op jit(solution)/shard_map/pallas_call | solution.py:419
  419.0 6.4 %collective-permute-start.10 = (bf16[1536,128]{1,0:T(8,128)(2,1)}, bf16[1536,128]{1,0:T(8,128)(2,1)S(1)}, u32[]{:S(2)}, u32[]{:S(2)}) collective-permute-start(bf16[1536,128]{1,0:T(8,128)(2,1)} %bitcast.63), channel_id=1, source_target_pairs={{0,16},{2,18},{4,20},{6,22},{8,24},{10,26},{12,28},{14,30},{16,0},... | collective-permute-start | bytes 1179656 | tf_op jit(solution)/shard_map/ppermute | solution.py:569
  425.4 1.5 collective-permute-start.12
  426.9 0.6 collective-permute-start.13
  427.4 11.2 %collective-permute-done.10.refs_2_ = bf16[1536,128]{1,0:T(8,128)(2,1)S(1)} collective-permute-done((bf16[1536,128]{1,0:T(8,128)(2,1)}, bf16[1536,128]{1,0:T(8,128)(2,1)S(1)}, u32[]{:S(2)}, u32[]{:S(2)}) %collective-permute-start.10) | collective-permute-done | bytes 393248 | tf_op jit(solution)/shard_map/ppermute | solution.py:569
  438.6 1.7 collective-permute-start.11
  440.4 0.7 copy-done.14
  441.1 0.8 copy-done.15
  441.9 6.4 %shard_map.63.refs_2_ = f32[1536,512]{1,0:T(8,128)} custom-call(s32[3]{0:T(128)} %pad_add_fusion.place_ref, bf16[1536,128]{1,0:T(8,128)(2,1)} %bitcast.55, bf16[1536,128]{1,0:T(8,128)(2,1)} %copy-done.11, bf16[1536,128]{1,0:T(8,128)(2,1)} %copy-done.13, bf16[1536,128]{1,0:T(8,128)(2,1)} %copy-done.10, bf16[1536,128]{1,0:T(8,128)(2,1)} %copy-done.12, ...), custom_call_target="tpu_custom_call" | custom-call | flops 1 | bytes 1 | tf_op jit(solution)/shard_map/pallas_call | solution.py:471
  448.3 0.6 collective-permute-done.11.refs_0_
  448.9 0.7 copy-done.18
  449.6 5.1 %shard_map.64 = bf16[1536,512]{1,0:T(8,128)(2,1)} custom-call(s32[3]{0:T(128)} %pad_add_fusion.place_ref, bf16[1536,128]{1,0:T(8,128)(2,1)} %copy-done.18, bf16[512,512]{1,0:T(8,128)(2,1)} %copy-done.1, f32[1536,512]{1,0:T(8,128)} %shard_map.63.refs_2_), custom_call_target="tpu_custom_call" | custom-call | flops 1 | bytes 1 | tf_op jit(solution)/shard_map/pallas_call | solution.py:471
  (52 shorter events, 0.3 us)
Async XLA Ops:
  6.5 41.8 %all-gather.9.cloned.1.call-start = ((), (), s32[]{:S(2)}) async-start(), calls=%async_computation | async-start | bytes 3932160 | tf_op jit(solution)/shard_map/all_gather | solution.py:575
  6.5 1.9 copy-start.4
  6.5 2.4 copy-start.5
  10.5 7.5 %copy-start.19 = (s32[1024,2]{0,1:T(2,128)S(1)}, s32[1024,2]{0,1:T(2,128)}, u32[]{:S(2)}) copy-start(s32[1024,2]{0,1:T(2,128)} %param.8) | copy-start | bytes 24580
  10.5 14.3 %copy-start = (bf16[512,1024]{1,0:T(8,128)(2,1)S(1)}, bf16[512,1024]{1,0:T(8,128)(2,1)}, u32[]{:S(2)}) copy-start(bf16[512,1024]{1,0:T(8,128)(2,1)} %refs_10_.1) | copy-start | bytes 3145732
  11.5 73.2 %all-gather.11.cloned.1.call-start = ((), (), s32[]{:S(2)}) async-start(), calls=%async_computation.1 | async-start | bytes 3932160 | tf_op jit(solution)/shard_map/all_gather | solution.py:575
  12.5 34.7 %copy-start.17 = (bf16[1536,128]{1,0:T(8,128)(2,1)S(1)}, bf16[1536,128]{1,0:T(8,128)(2,1)}, u32[]{:S(2)}) copy-start(bf16[1536,128]{1,0:T(8,128)(2,1)} %get-tuple-element.98) | copy-start | bytes 1179652
  12.5 31.5 %collective-permute-start = (bf16[2,8,192,128]{3,2,1,0:T(8,128)(2,1)}, bf16[2,8,192,128]{3,2,1,0:T(8,128)(2,1)}, u32[]{:S(2)}, u32[]{:S(2)}) collective-permute-start(bf16[2,8,192,128]{3,2,1,0:T(8,128)(2,1)} %pad_maximum_fusion), channel_id=1, source_target_pairs={{0,8},{2,10},{4,12},{6,14},{8,0},{10,2},{12,4},{14,6},{16,24},{18,... | collective-permute-start | bytes 2359304 | tf_op jit(solution)/shard_map/ppermute | solution.py:569
  15.5 28.5 %collective-permute-start.1 = (bf16[8,192,128]{2,1,0:T(8,128)(2,1)}, bf16[8,192,128]{2,1,0:T(8,128)(2,1)S(1)}, u32[]{:S(2)}, u32[]{:S(2)}) collective-permute-start(bf16[8,192,128]{2,1,0:T(8,128)(2,1)} %bitcast.58), channel_id=1, source_target_pairs={{0,24},{2,26},{4,28},{6,30},{8,16},{10,18},{12,20},{14,22},{16,8},... | collective-permute-start | bytes 1179656 | tf_op jit(solution)/shard_map/ppermute | solution.py:569
  44.0 4.9 %copy-start.2 = (bf16[8,192,128]{2,1,0:T(8,128)(2,1)}, bf16[8,192,128]{2,1,0:T(8,128)(2,1)S(1)}, u32[]{:S(2)}) copy-start(bf16[8,192,128]{2,1,0:T(8,128)(2,1)S(1)} %collective-permute-done.1.refs_1_) | copy-start | bytes 1179652
  44.1 77.9 %all-gather.13.cloned.1.call-start = ((), (), s32[]{:S(2)}) async-start(), calls=%async_computation.2 | async-start | bytes 3932160 | tf_op jit(solution)/shard_map/all_gather | solution.py:575
  44.1 39.1 %collective-permute-start.2 = (bf16[2,8,192,128]{3,2,1,0:T(8,128)(2,1)}, bf16[2,8,192,128]{3,2,1,0:T(8,128)(2,1)S(1)}, u32[]{:S(2)}, u32[]{:S(2)}) collective-permute-start(bf16[2,8,192,128]{3,2,1,0:T(8,128)(2,1)} %pad_maximum_fusion.1), channel_id=1, source_target_pairs={{0,24},{2,26},{4,28},{6,30},{8,16},{10,18},{12,20},{14,22},{16,8},... | collective-permute-start | bytes 2359304 | tf_op jit(solution)/shard_map/ppermute | solution.py:569
  45.7 27.3 %collective-permute-start.4 = (bf16[512,512]{1,0:T(8,128)(2,1)}, bf16[512,512]{1,0:T(8,128)(2,1)S(1)}, u32[]{:S(2)}, u32[]{:S(2)}) collective-permute-start(bf16[512,512]{1,0:T(8,128)(2,1)} %constant_dynamic-slice_fusion.6), channel_id=1, source_target_pairs={{0,1},{1,0},{2,3},{3,2},{4,5},{5,4},{6,7},{7,6},{8,9},{9,8},{10,11... | collective-permute-start | bytes 1572872 | tf_op jit(solution)/shard_map/ppermute | solution.py:578
  47.3 25.8 %collective-permute-start.3 = (bf16[8,192,128]{2,1,0:T(8,128)(2,1)S(1)}, bf16[8,192,128]{2,1,0:T(8,128)(2,1)S(1)}, u32[]{:S(2)}, u32[]{:S(2)}) collective-permute-start(bf16[8,192,128]{2,1,0:T(8,128)(2,1)S(1)} %bitcast.57), channel_id=1, source_target_pairs={{0,8},{2,10},{4,12},{6,14},{8,0},{10,2},{12,4},{14,6},{16,24},{18,... | collective-permute-start | bytes 1179656 | tf_op jit(solution)/shard_map/ppermute | solution.py:569
  65.0 19.1 %copy-start.8 = (bf16[2,8,192,128]{3,2,1,0:T(8,128)(2,1)S(1)}, bf16[2,8,192,128]{3,2,1,0:T(8,128)(2,1)}, u32[]{:S(2)}) copy-start(bf16[2,8,192,128]{3,2,1,0:T(8,128)(2,1)} %pad_maximum_fusion.2) | copy-start | bytes 2359300
  73.1 0.8 copy-start.3
  73.1 35.1 %copy-start.1 = (bf16[512,512]{1,0:T(8,128)(2,1)}, bf16[512,512]{1,0:T(8,128)(2,1)S(1)}, u32[]{:S(2)}) copy-start(bf16[512,512]{1,0:T(8,128)(2,1)S(1)} %collective-permute-done.4.refs_11_.refs_12_.refs_13_.refs_1_) | copy-start | bytes 1572868
  83.2 0.9 copy-start.7
  84.1 75.7 %all-gather.15.cloned.1.call-start = ((), (), s32[]{:S(2)}) async-start(), calls=%async_computation.3 | async-start | bytes 3932160 | tf_op jit(solution)/shard_map/all_gather | solution.py:575
  84.1 36.8 %collective-permute-start.5 = (bf16[2,8,192,128]{3,2,1,0:T(8,128)(2,1)S(1)}, bf16[2,8,192,128]{3,2,1,0:T(8,128)(2,1)S(1)}, u32[]{:S(2)}, u32[]{:S(2)}) collective-permute-start(bf16[2,8,192,128]{3,2,1,0:T(8,128)(2,1)S(1)} %copy-done.8), channel_id=1, source_target_pairs={{0,16},{2,18},{4,20},{6,22},{8,24},{10,26},{12,28},{14,30},{16,0},... | collective-permute-start | bytes 2359304 | tf_op jit(solution)/shard_map/ppermute | solution.py:569
  84.8 37.1 %copy-start.16 = (bf16[1536,128]{1,0:T(8,128)(2,1)S(1)}, bf16[1536,128]{1,0:T(8,128)(2,1)}, u32[]{:S(2)}) copy-start(bf16[1536,128]{1,0:T(8,128)(2,1)} %get-tuple-element.97) | copy-start | bytes 1179652
  120.9 0.9 copy-start.9
  121.9 22.5 %collective-permute-start.6 = (bf16[8,192,128]{2,1,0:T(8,128)(2,1)S(1)}, bf16[8,192,128]{2,1,0:T(8,128)(2,1)S(1)}, u32[]{:S(2)}, u32[]{:S(2)}) collective-permute-start(bf16[8,192,128]{2,1,0:T(8,128)(2,1)S(1)} %bitcast.56), channel_id=1, source_target_pairs={{0,16},{2,18},{4,20},{6,22},{8,24},{10,26},{12,28},{14,30},{16,0},... | collective-permute-start | bytes 1179656 | tf_op jit(solution)/shard_map/ppermute | solution.py:569
  144.4 0.8 copy-start.6
  346.1 72.8 %collective-permute-start.7 = (bf16[1536,128]{1,0:T(8,128)(2,1)}, bf16[1536,128]{1,0:T(8,128)(2,1)S(1)}, u32[]{:S(2)}, u32[]{:S(2)}) collective-permute-start(bf16[1536,128]{1,0:T(8,128)(2,1)} %bitcast.62), channel_id=1, source_target_pairs={{0,24},{2,26},{4,28},{6,30},{8,16},{10,18},{12,20},{14,22},{16,8},... | collective-permute-start | bytes 1179656 | tf_op jit(solution)/shard_map/ppermute | solution.py:569
  346.1 72.8 %collective-permute-start.8 = (bf16[1536,128]{1,0:T(8,128)(2,1)}, bf16[1536,128]{1,0:T(8,128)(2,1)S(1)}, u32[]{:S(2)}, u32[]{:S(2)}) collective-permute-start(bf16[1536,128]{1,0:T(8,128)(2,1)} %bitcast.61), channel_id=1, source_target_pairs={{0,8},{2,10},{4,12},{6,14},{8,0},{10,2},{12,4},{14,6},{16,24},{18,... | collective-permute-start | bytes 1179656 | tf_op jit(solution)/shard_map/ppermute | solution.py:569
  348.4 70.5 %collective-permute-start.9 = (bf16[1536,128]{1,0:T(8,128)(2,1)}, bf16[1536,128]{1,0:T(8,128)(2,1)S(1)}, u32[]{:S(2)}, u32[]{:S(2)}) collective-permute-start(bf16[1536,128]{1,0:T(8,128)(2,1)} %bitcast.54), channel_id=1, source_target_pairs={{0,1},{1,0},{2,3},{3,2},{4,5},{5,4},{6,7},{7,6},{8,9},{9,8},{10,11... | collective-permute-start | bytes 1179656 | tf_op jit(solution)/shard_map/ppermute | solution.py:578
  418.9 21.5 %copy-start.10 = (bf16[1536,128]{1,0:T(8,128)(2,1)}, bf16[1536,128]{1,0:T(8,128)(2,1)S(1)}, u32[]{:S(2)}) copy-start(bf16[1536,128]{1,0:T(8,128)(2,1)S(1)} %collective-permute-done.7.refs_3_) | copy-start | bytes 1179652
  418.9 21.5 %copy-start.11 = (bf16[1536,128]{1,0:T(8,128)(2,1)}, bf16[1536,128]{1,0:T(8,128)(2,1)S(1)}, u32[]{:S(2)}) copy-start(bf16[1536,128]{1,0:T(8,128)(2,1)S(1)} %collective-permute-done.8.refs_1_) | copy-start | bytes 1179652
  419.0 21.4 %copy-start.12 = (bf16[1536,128]{1,0:T(8,128)(2,1)}, bf16[1536,128]{1,0:T(8,128)(2,1)S(1)}, u32[]{:S(2)}) copy-start(bf16[1536,128]{1,0:T(8,128)(2,1)S(1)} %collective-permute-done.9.refs_4_) | copy-start | bytes 1179652
  419.0 19.6 %collective-permute-start.10 = (bf16[1536,128]{1,0:T(8,128)(2,1)}, bf16[1536,128]{1,0:T(8,128)(2,1)S(1)}, u32[]{:S(2)}, u32[]{:S(2)}) collective-permute-start(bf16[1536,128]{1,0:T(8,128)(2,1)} %bitcast.63), channel_id=1, source_target_pairs={{0,16},{2,18},{4,20},{6,22},{8,24},{10,26},{12,28},{14,30},{16,0},... | collective-permute-start | bytes 1179656 | tf_op jit(solution)/shard_map/ppermute | solution.py:569
  425.4 15.0 %collective-permute-start.12 = (bf16[1536,128]{1,0:T(8,128)(2,1)S(1)}, bf16[1536,128]{1,0:T(8,128)(2,1)S(1)}, u32[]{:S(2)}, u32[]{:S(2)}) collective-permute-start(bf16[1536,128]{1,0:T(8,128)(2,1)S(1)} %collective-permute-done.8.refs_1_), channel_id=1, source_target_pairs={{0,1},{1,0},{2,3},{3,2},{4,5},{5,4},{6,7},{7,6},{8,9},{9,8},{10,11... | collective-permute-start | bytes 1179656 | tf_op jit(solution)/shard_map/ppermute | solution.py:578
  426.9 13.5 %collective-permute-start.13 = (bf16[1536,128]{1,0:T(8,128)(2,1)S(1)}, bf16[1536,128]{1,0:T(8,128)(2,1)S(1)}, u32[]{:S(2)}, u32[]{:S(2)}) collective-permute-start(bf16[1536,128]{1,0:T(8,128)(2,1)S(1)} %collective-permute-done.7.refs_3_), channel_id=1, source_target_pairs={{0,1},{1,0},{2,3},{3,2},{4,5},{5,4},{6,7},{7,6},{8,9},{9,8},{10,11... | collective-permute-start | bytes 1179656 | tf_op jit(solution)/shard_map/ppermute | solution.py:578
  438.6 1.8 copy-start.13
  438.6 10.3 %collective-permute-start.11 = (bf16[1536,128]{1,0:T(8,128)(2,1)S(1)}, bf16[1536,128]{1,0:T(8,128)(2,1)S(1)}, u32[]{:S(2)}, u32[]{:S(2)}) collective-permute-start(bf16[1536,128]{1,0:T(8,128)(2,1)S(1)} %collective-permute-done.10.refs_2_), channel_id=1, source_target_pairs={{0,1},{1,0},{2,3},{3,2},{4,5},{5,4},{6,7},{7,6},{8,9},{9,8},{10,11... | collective-permute-start | bytes 1179656 | tf_op jit(solution)/shard_map/ppermute | solution.py:578
  440.4 0.8 copy-start.14
  441.1 0.8 copy-start.15
  448.9 0.7 copy-start.18
Sparse Core Ops, SparseCore 0:
  11.6 31.2 all-gather.8
  44.5 28.6 all-gather.10
  84.2 27.5 all-gather.12
  122.0 27.1 all-gather.14

commit v4 on v3

--- a/solution.py
+++ b/solution.py
@@ -18,6 +18,7 @@
 LOW, HIGH = 2.0**-60, 2.0**100
 NEVER = -1e30
 VMEM_LIMIT = 60 * 1024 * 1024
+PROJECT_LIMIT = 16 * 1024 * 1024
 
 
 def table_kernel(planes, plane_size, group, frames_here, place_ref, ends_ref, table_ref):
@@ -479,7 +480,7 @@
             out_specs=kept,
         ),
         out_shape=jax.ShapeDtypeStruct((rows, columns), near.dtype if ends else jnp.float32),
-        compiler_params=pltpu.CompilerParams(vmem_limit_bytes=VMEM_LIMIT),
+        compiler_params=pltpu.CompilerParams(vmem_limit_bytes=PROJECT_LIMIT),
         cost_estimate=pl.CostEstimate(flops=1, bytes_accessed=1, transcendentals=0),
     )(
         places,
@@ -514,23 +515,23 @@
 
     keyed = [gathered(0), None, None, None]
     pairs[1], queries[3] = swap(pairs[1], 1), swap(queries[3], 3)
-    pairs[1], queries[3], queries[1], pairs[3], table, far, order = barrier(
-        (pairs[1], queries[3], queries[1], pairs[3], table, far, order)
+    pairs[1], queries[3], queries[1], pairs[3], table, order = barrier(
+        (pairs[1], queries[3], queries[1], pairs[3], table, order)
     )
     keyed[1] = gathered(1)
-    pairs[3], queries[1], far = swap(pairs[3], 3), swap(queries[1], 1), across(far)
+    pairs[3], queries[1] = swap(pairs[3], 3), swap(queries[1], 1)
     order, *early = run([0, 3], 0, keyed, [])
-    queries[1], far, order = barrier((queries[1], far, order))
-    order, *late = run([1], 0, keyed, [])
-    pairs[3], pairs[2], order = barrier((pairs[3], pairs[2], order))
+    queries[1], pairs[3], pairs[2], order = barrier((queries[1], pairs[3], pairs[2], order))
     keyed[3] = gathered(3)
     pairs[2] = swap(pairs[2], 2)
+    order, *late = run([1], 0, keyed, [])
     order, *state = run([0, 3, 1], 1, keyed, [early, late])
-    pairs[2], queries[2], order = barrier((pairs[2], queries[2], order))
+    pairs[2], queries[2], far, order = barrier((pairs[2], queries[2], far, order))
     keyed[2] = gathered(2)
     queries[2] = swap(queries[2], 2)
     order, *state = run([0, 3, 1], 3, keyed, [state])
-    queries[2], order = barrier((queries[2], order))
+    queries[2], far, order = barrier((queries[2], far, order))
+    far = across(far)
     order, *last = run([2], 0, keyed, [], number=2)
     merged, others = [None] * 4, [None] * 4
 
@@ -541,8 +542,8 @@
     merged[0], out, near_out, order = barrier(tuple(map(rows_of, outs)) + (order,))
     merged[3], merged[1], others[0] = swap(out, 3), swap(near_out, 1), across(merged[0])
     order, out = run([2], 2, keyed, [last], True, 2)
-    out, merged[3], merged[1], others[0] = barrier(
-        (rows_of(out), merged[3], merged[1], others[0])
+    out, merged[3], merged[1], others[0], far = barrier(
+        (rows_of(out), merged[3], merged[1], others[0], far)
     )
     merged[2], others[1], others[3] = swap(out, 2), across(merged[1]), across(merged[3])
     others[2] = across(merged[2])

time: 460 us -> 447 us (0.972); the launches traced: 461 us -> 442 us
  waiting for transfers between devices: 50 us -> 42.1 us
  Pallas kernels: 358 us -> 353 us
    ppermute x9, waiting for transfers between devices: 49.3 us -> 38.5 us  [swap(): lax.ppermute(array, 'frames', [(index, index ^ distance * axis) for index...]
    pallas_call x2, Pallas kernels: 11.5 us -> 5.8 us  [project(): pl.pallas_call(functools.partial(project_kernel, len(parts)), grid_spec=p...]
  transfers between devices with their start and end apart: 18 -> 18, of which waited for: 5 -> 6; matrix products, arithmetic and copies ran while one was open for 1% -> 1% of each run, Pallas kernels for 36% -> 79%
where the time goes in v4:
time: 447 us; the launch traced here: 442 us
  Pallas kernels  353 us (79%)
  waiting for transfers between devices  42.1 us (9%)
  starting transfers between devices  22.5 us (5%)
  between operations  13.3 us (3%)
  local copies, waits for them, and re-layouts  7.97 us (2%)
    pallas_call x7, Pallas kernels, attend(): pl.pallas_call(functools.partial(attend_kernel, begin, number, tuple(chun...  341 us
    ppermute x9, waiting for transfers between devices, swap(): lax.ppermute(array, 'frames', [(index, index ^ distance * axis) for index...  38.5 us
    ppermute x9, starting transfers between devices, swap(): lax.ppermute(array, 'frames', [(index, index ^ distance * axis) for index...  16.8 us
  transfers between devices with their start and end apart: 18, of which 6 were waited for; matrix products, arithmetic and copies ran while one was open for 1% of the time, Pallas kernels for 79%

profile of v4, /device:TPU:0, one launch (start us, length us, event | category | flops | bytes accessed | tf_op | source)
XLA Modules:
  0.0 442.4 jit_solution(14496838586369997670)
XLA Ops:
  6.5 2.4 constant_dynamic-slice_fusion.3
  8.9 1.6 constant_dynamic-slice_fusion.1
  10.6 0.9 pad_maximum_fusion.3
  11.5 0.0 all-gather.11.cloned.1.call-start
  11.6 0.0 copy-done.7
  11.6 0.1 pad_maximum_fusion
  11.7 3.1 collective-permute-start
  14.8 2.5 collective-permute-start.1
  17.3 0.6 copy.8
  17.9 0.7 pad_add_fusion.place_ref
  18.5 5.6 %shard_map.55.table_ref = s32[4,2,256]{2,1,0:T(2,128)} custom-call(s32[3]{0:T(128)} %pad_add_fusion.place_ref, s32[2,8,128]{2,1,0:T(8,128)} %bitcast.59), custom_call_target="tpu_custom_call" | custom-call | tf_op jit(solution)/shard_map/pallas_call | solution.py:131
  24.2 1.0 pad_maximum_fusion.1
  25.1 17.9 %collective-permute-done.1.refs_1_ = bf16[8,192,128]{2,1,0:T(8,128)(2,1)S(1)} collective-permute-done((bf16[8,192,128]{2,1,0:T(8,128)(2,1)}, bf16[8,192,128]{2,1,0:T(8,128)(2,1)S(1)}, u32[]{:S(2)}, u32[]{:S(2)}) %collective-permute-start.1) | collective-permute-done | bytes 393248 | tf_op jit(solution)/shard_map/ppermute | solution.py:570
  43.1 0.9 copy-done.9
  44.0 0.0 all-gather.13.cloned.1.call-start
  44.1 1.5 collective-permute-start.3
  45.6 0.9 pad_maximum_fusion.2
  46.6 0.6 broadcast_in_dim.3.order_ref
  47.2 15.6 %shard_map.56 = (s32[8,128]{1,0:T(8,128)}, f32[16,192,128]{2,1,0:T(8,128)}, f32[16,192,128]{2,1,0:T(8,128)}) custom-call(s32[4,2,256]{2,1,0:T(2,128)} %shard_map.55.table_ref, s32[3]{0:T(128)} %pad_add_fusion.place_ref, s32[8,128]{1,0:T(8,128)} %broadcast_in_dim.3.order_ref, bf16[8,192,128]{2,1,0:T(8,128)(2,1)} %bitcast.44, bf16[8,192,128]{2,1,0:T(8,128)(2,1)} %copy-done.3, ...), custom_call_target="tpu_custom_call" | custom-call | flops 1 | bytes 1 | tf_op jit(solution)/shard_map/pallas_call | solution.py:420
  62.8 9.5 %collective-permute-done.2.refs_0_.refs_2_ = bf16[8,192,128]{2,1,0:T(8,128)(2,1)S(1)} collective-permute-done((bf16[8,192,128]{2,1,0:T(8,128)(2,1)}, bf16[8,192,128]{2,1,0:T(8,128)(2,1)S(1)}, u32[]{:S(2)}, u32[]{:S(2)}) %collective-permute-start.2) | collective-permute-done | bytes 393248 | tf_op jit(solution)/shard_map/ppermute | solution.py:570
  72.3 0.0 all-gather.15.cloned.1.call-start
  72.3 5.1 %collective-permute-start.4 = (bf16[2,8,192,128]{3,2,1,0:T(8,128)(2,1)S(1)}, bf16[2,8,192,128]{3,2,1,0:T(8,128)(2,1)S(1)}, u32[]{:S(2)}, u32[]{:S(2)}) collective-permute-start(bf16[2,8,192,128]{3,2,1,0:T(8,128)(2,1)S(1)} %copy-done.11), channel_id=1, source_target_pairs={{0,16},{2,18},{4,20},{6,22},{8,24},{10,26},{12,28},{14,30},{16,0},... | collective-permute-start | bytes 2359304 | tf_op jit(solution)/shard_map/ppermute | solution.py:570
  77.4 0.9 constant_dynamic-slice_fusion
  78.3 9.8 %shard_map.57 = (s32[8,128]{1,0:T(8,128)}, f32[8,192,128]{2,1,0:T(8,128)}, f32[8,192,128]{2,1,0:T(8,128)}) custom-call(s32[4,2,256]{2,1,0:T(2,128)} %shard_map.55.table_ref, s32[3]{0:T(128)} %pad_add_fusion.place_ref, s32[8,128]{1,0:T(8,128)} %get-tuple-element.58.order_ref, bf16[8,192,128]{2,1,0:T(8,128)(2,1)} %copy-done.4, ...), custom_call_target="tpu_custom_call" | custom-call | flops 1 | bytes 1 | tf_op jit(solution)/shard_map/pallas_call | solution.py:420
  88.1 0.0 all-gather.11.cloned.1.call-done
  88.1 23.4 %shard_map.58 = (s32[8,128]{1,0:T(8,128)}, f32[24,192,128]{2,1,0:T(8,128)}, f32[24,192,128]{2,1,0:T(8,128)}) custom-call(s32[4,2,256]{2,1,0:T(2,128)} %shard_map.55.table_ref, s32[3]{0:T(128)} %pad_add_fusion.place_ref, s32[8,128]{1,0:T(8,128)} %get-tuple-element.60.order_ref, bf16[8,192,128]{2,1,0:T(8,128)(2,1)} %bitcast.45, ...), custom_call_target="tpu_custom_call" | custom-call | flops 1 | bytes 1 | tf_op jit(solution)/shard_map/pallas_call | solution.py:420
  111.5 0.5 collective-permute-done.4
  112.0 0.9 copy-done.10
  112.9 0.1 collective-permute-start.5
  113.0 0.0 all-gather.13.cloned.1.call-done
  113.0 22.4 %shard_map.59 = (s32[8,128]{1,0:T(8,128)}, f32[24,192,128]{2,1,0:T(8,128)}, f32[24,192,128]{2,1,0:T(8,128)}) custom-call(s32[4,2,256]{2,1,0:T(2,128)} %shard_map.55.table_ref, s32[3]{0:T(128)} %pad_add_fusion.place_ref, s32[8,128]{1,0:T(8,128)} %get-tuple-element.69.order_ref, bf16[8,192,128]{2,1,0:T(8,128)(2,1)} %bitcast.46, ...), custom_call_target="tpu_custom_call" | custom-call | flops 1 | bytes 1 | tf_op jit(solution)/shard_map/pallas_call | solution.py:420
  135.5 1.6 collective-permute-start.9
  137.1 14.6 %shard_map.60 = (s32[8,128]{1,0:T(8,128)}, f32[8,192,128]{2,1,0:T(8,128)}, f32[8,192,128]{2,1,0:T(8,128)}) custom-call(s32[4,2,256]{2,1,0:T(2,128)} %shard_map.55.table_ref, s32[3]{0:T(128)} %pad_add_fusion.place_ref, s32[8,128]{1,0:T(8,128)} %get-tuple-element.74.order_ref, bf16[8,192,128]{2,1,0:T(8,128)(2,1)} %copy-done.8, ...), custom_call_target="tpu_custom_call" | custom-call | flops 1 | bytes 1 | tf_op jit(solution)/shard_map/pallas_call | solution.py:420
  151.6 0.0 all-gather.15.cloned.1.call-done
  151.7 184.5 %shard_map.61 = (s32[8,128]{1,0:T(8,128)}, bf16[8,192,128]{2,1,0:T(8,128)(2,1)}, bf16[8,192,128]{2,1,0:T(8,128)(2,1)}, bf16[8,192,128]{2,1,0:T(8,128)(2,1)}) custom-call(s32[4,2,256]{2,1,0:T(2,128)} %shard_map.55.table_ref, s32[3]{0:T(128)} %pad_add_fusion.place_ref, s32[8,128]{1,0:T(8,128)} %get-tuple-element.76.order_ref, bf16[8,192,128]{2,1,0:T(8,128)(2,1)} %bitcast.47, ...), custom_call_target="tpu_custom_call" | custom-call | flops 1 | bytes 1 | tf_op jit(solution)/shard_map/pallas_call | solution.py:420
  336.1 3.0 collective-permute-start.6
  339.1 1.0 collective-permute-start.7
  340.2 0.7 collective-permute-start.8
  340.9 71.2 %shard_map.62 = (s32[8,128]{1,0:T(8,128)}, bf16[8,192,128]{2,1,0:T(8,128)(2,1)}) custom-call(s32[4,2,256]{2,1,0:T(2,128)} %shard_map.55.table_ref, s32[3]{0:T(128)} %pad_add_fusion.place_ref, s32[8,128]{1,0:T(8,128)} %get-tuple-element.84.order_ref, bf16[8,192,128]{2,1,0:T(8,128)(2,1)} %copy-done.8, bf16[4,2,8,192,128]{4,3,2,1,0:T(8,128)(2,1)} %bitcast.34, ...), custom_call_target="tpu_custom_call" | custom-call | flops 1 | bytes 1 | tf_op jit(solution)/shard_map/pallas_call | solution.py:420
  412.1 0.5 collective-permute-start.10
  412.6 1.3 collective-permute-start.12
  413.9 0.7 collective-permute-start.13
  414.6 10.7 %collective-permute-done.10.refs_2_ = bf16[1536,128]{1,0:T(8,128)(2,1)S(1)} collective-permute-done((bf16[1536,128]{1,0:T(8,128)(2,1)}, bf16[1536,128]{1,0:T(8,128)(2,1)S(1)}, u32[]{:S(2)}, u32[]{:S(2)}) %collective-permute-start.10) | collective-permute-done | bytes 393248 | tf_op jit(solution)/shard_map/ppermute | solution.py:570
  425.3 1.3 collective-permute-start.11
  426.6 2.3 collective-permute-done.13.refs_6_
  428.9 3.0 shard_map.63.refs_2_
  431.9 1.2 collective-permute-done.11.refs_0_
  433.1 2.8 shard_map.64
  (40 shorter events, 0.2 us)
Async XLA Ops:
  6.5 2.4 copy-start.5
  6.5 40.0 %all-gather.9.cloned.1.call-start = ((), (), s32[]{:S(2)}) async-start(), calls=%async_computation | async-start | bytes 3932160 | tf_op jit(solution)/shard_map/all_gather | solution.py:576
  6.5 2.4 copy-start.6
  10.6 1.1 copy-start.7
  10.6 6.7 %copy-start.13 = (s32[1024,2]{0,1:T(2,128)S(1)}, s32[1024,2]{0,1:T(2,128)}, u32[]{:S(2)}) copy-start(s32[1024,2]{0,1:T(2,128)} %param.8) | copy-start | bytes 24580
  11.5 76.6 %all-gather.11.cloned.1.call-start = ((), (), s32[]{:S(2)}) async-start(), calls=%async_computation.1 | async-start | bytes 3932160 | tf_op jit(solution)/shard_map/all_gather | solution.py:576
  11.7 31.4 %collective-permute-start = (bf16[2,8,192,128]{3,2,1,0:T(8,128)(2,1)S(1)}, bf16[2,8,192,128]{3,2,1,0:T(8,128)(2,1)S(1)}, u32[]{:S(2)}, u32[]{:S(2)}) collective-permute-start(bf16[2,8,192,128]{3,2,1,0:T(8,128)(2,1)S(1)} %pad_maximum_fusion), channel_id=1, source_target_pairs={{0,8},{2,10},{4,12},{6,14},{8,0},{10,2},{12,4},{14,6},{16,24},{18,... | collective-permute-start | bytes 2359304 | tf_op jit(solution)/shard_map/ppermute | solution.py:570
  14.8 28.3 %collective-permute-start.1 = (bf16[8,192,128]{2,1,0:T(8,128)(2,1)}, bf16[8,192,128]{2,1,0:T(8,128)(2,1)S(1)}, u32[]{:S(2)}, u32[]{:S(2)}) collective-permute-start(bf16[8,192,128]{2,1,0:T(8,128)(2,1)} %bitcast.58), channel_id=1, source_target_pairs={{0,24},{2,26},{4,28},{6,30},{8,16},{10,18},{12,20},{14,22},{16,8},... | collective-permute-start | bytes 1179656 | tf_op jit(solution)/shard_map/ppermute | solution.py:570
  43.1 4.1 copy-start.3
  43.1 0.9 copy-start.9
  44.0 69.0 %all-gather.13.cloned.1.call-start = ((), (), s32[]{:S(2)}) async-start(), calls=%async_computation.2 | async-start | bytes 3932160 | tf_op jit(solution)/shard_map/all_gather | solution.py:576
  44.1 28.2 %collective-permute-start.3 = (bf16[2,8,192,128]{3,2,1,0:T(8,128)(2,1)}, bf16[2,8,192,128]{3,2,1,0:T(8,128)(2,1)}, u32[]{:S(2)}, u32[]{:S(2)}) collective-permute-start(bf16[2,8,192,128]{3,2,1,0:T(8,128)(2,1)} %pad_maximum_fusion.1), channel_id=1, source_target_pairs={{0,24},{2,26},{4,28},{6,30},{8,16},{10,18},{12,20},{14,22},{16,8},... | collective-permute-start | bytes 2359304 | tf_op jit(solution)/shard_map/ppermute | solution.py:570
  45.6 26.6 %collective-permute-start.2 = (bf16[8,192,128]{2,1,0:T(8,128)(2,1)}, bf16[8,192,128]{2,1,0:T(8,128)(2,1)S(1)}, u32[]{:S(2)}, u32[]{:S(2)}) collective-permute-start(bf16[8,192,128]{2,1,0:T(8,128)(2,1)} %bitcast.57), channel_id=1, source_target_pairs={{0,8},{2,10},{4,12},{6,14},{8,0},{10,2},{12,4},{14,6},{16,24},{18,... | collective-permute-start | bytes 1179656 | tf_op jit(solution)/shard_map/ppermute | solution.py:570
  47.2 25.2 %copy-start.11 = (bf16[2,8,192,128]{3,2,1,0:T(8,128)(2,1)S(1)}, bf16[2,8,192,128]{3,2,1,0:T(8,128)(2,1)}, u32[]{:S(2)}) copy-start(bf16[2,8,192,128]{3,2,1,0:T(8,128)(2,1)} %pad_maximum_fusion.2) | copy-start | bytes 2359300
  47.2 30.2 %copy-start = (bf16[512,1024]{1,0:T(8,128)(2,1)S(1)}, bf16[512,1024]{1,0:T(8,128)(2,1)}, u32[]{:S(2)}) copy-start(bf16[512,1024]{1,0:T(8,128)(2,1)} %refs_10_.1) | copy-start | bytes 3145732
  72.2 6.0 %copy-start.4 = (bf16[8,192,128]{2,1,0:T(8,128)(2,1)}, bf16[8,192,128]{2,1,0:T(8,128)(2,1)S(1)}, u32[]{:S(2)}) copy-start(bf16[8,192,128]{2,1,0:T(8,128)(2,1)S(1)} %collective-permute-done.2.refs_0_.refs_2_) | copy-start | bytes 1179652
  72.3 79.4 %all-gather.15.cloned.1.call-start = ((), (), s32[]{:S(2)}) async-start(), calls=%async_computation.3 | async-start | bytes 3932160 | tf_op jit(solution)/shard_map/all_gather | solution.py:576
  72.3 39.6 %collective-permute-start.4 = (bf16[2,8,192,128]{3,2,1,0:T(8,128)(2,1)S(1)}, bf16[2,8,192,128]{3,2,1,0:T(8,128)(2,1)S(1)}, u32[]{:S(2)}, u32[]{:S(2)}) collective-permute-start(bf16[2,8,192,128]{3,2,1,0:T(8,128)(2,1)S(1)} %copy-done.11), channel_id=1, source_target_pairs={{0,16},{2,18},{4,20},{6,22},{8,24},{10,26},{12,28},{14,30},{16,0},... | collective-permute-start | bytes 2359304 | tf_op jit(solution)/shard_map/ppermute | solution.py:570
  88.1 24.8 %copy-start.12 = (bf16[1536,128]{1,0:T(8,128)(2,1)S(1)}, bf16[1536,128]{1,0:T(8,128)(2,1)}, u32[]{:S(2)}) copy-start(bf16[1536,128]{1,0:T(8,128)(2,1)} %get-tuple-element.97) | copy-start | bytes 1179652
  112.0 0.9 copy-start.10
  112.9 22.6 %collective-permute-start.5 = (bf16[8,192,128]{2,1,0:T(8,128)(2,1)S(1)}, bf16[8,192,128]{2,1,0:T(8,128)(2,1)S(1)}, u32[]{:S(2)}, u32[]{:S(2)}) collective-permute-start(bf16[8,192,128]{2,1,0:T(8,128)(2,1)S(1)} %bitcast.56), channel_id=1, source_target_pairs={{0,16},{2,18},{4,20},{6,22},{8,24},{10,26},{12,28},{14,30},{16,0},... | collective-permute-start | bytes 1179656 | tf_op jit(solution)/shard_map/ppermute | solution.py:570
  135.5 1.6 copy-start.8
  135.5 276.6 %collective-permute-start.9 = (bf16[512,512]{1,0:T(8,128)(2,1)}, bf16[512,512]{1,0:T(8,128)(2,1)S(1)}, u32[]{:S(2)}, u32[]{:S(2)}) collective-permute-start(bf16[512,512]{1,0:T(8,128)(2,1)} %constant_dynamic-slice_fusion), channel_id=1, source_target_pairs={{0,1},{1,0},{2,3},{3,2},{4,5},{5,4},{6,7},{7,6},{8,9},{9,8},{10,11... | collective-permute-start | bytes 1572872 | tf_op jit(solution)/shard_map/ppermute | solution.py:579
  336.1 75.9 %collective-permute-start.6 = (bf16[1536,128]{1,0:T(8,128)(2,1)}, bf16[1536,128]{1,0:T(8,128)(2,1)S(1)}, u32[]{:S(2)}, u32[]{:S(2)}) collective-permute-start(bf16[1536,128]{1,0:T(8,128)(2,1)} %bitcast.62), channel_id=1, source_target_pairs={{0,24},{2,26},{4,28},{6,30},{8,16},{10,18},{12,20},{14,22},{16,8},... | collective-permute-start | bytes 1179656 | tf_op jit(solution)/shard_map/ppermute | solution.py:570
  339.1 73.0 %collective-permute-start.7 = (bf16[1536,128]{1,0:T(8,128)(2,1)}, bf16[1536,128]{1,0:T(8,128)(2,1)S(1)}, u32[]{:S(2)}, u32[]{:S(2)}) collective-permute-start(bf16[1536,128]{1,0:T(8,128)(2,1)} %bitcast.61), channel_id=1, source_target_pairs={{0,8},{2,10},{4,12},{6,14},{8,0},{10,2},{12,4},{14,6},{16,24},{18,... | collective-permute-start | bytes 1179656 | tf_op jit(solution)/shard_map/ppermute | solution.py:570
  340.2 71.9 %collective-permute-start.8 = (bf16[1536,128]{1,0:T(8,128)(2,1)}, bf16[1536,128]{1,0:T(8,128)(2,1)S(1)}, u32[]{:S(2)}, u32[]{:S(2)}) collective-permute-start(bf16[1536,128]{1,0:T(8,128)(2,1)} %bitcast.28), channel_id=1, source_target_pairs={{0,1},{1,0},{2,3},{3,2},{4,5},{5,4},{6,7},{7,6},{8,9},{9,8},{10,11... | collective-permute-start | bytes 1179656 | tf_op jit(solution)/shard_map/ppermute | solution.py:579
  340.9 88.0 %copy-start.1 = (bf16[8,192,128]{2,1,0:T(8,128)(2,1)S(1)}, bf16[8,192,128]{2,1,0:T(8,128)(2,1)}, u32[]{:S(2)}) copy-start(bf16[8,192,128]{2,1,0:T(8,128)(2,1)} %get-tuple-element.80) | copy-start | bytes 1179652
  340.9 88.0 %copy-start.2 = (s32[3]{0:T(128)S(1)}, s32[3]{0:T(128)}, u32[]{:S(2)}) copy-start(s32[3]{0:T(128)} %pad_add_fusion.place_ref) | copy-start | bytes 40
  412.1 13.2 %collective-permute-start.10 = (bf16[1536,128]{1,0:T(8,128)(2,1)}, bf16[1536,128]{1,0:T(8,128)(2,1)S(1)}, u32[]{:S(2)}, u32[]{:S(2)}) collective-permute-start(bf16[1536,128]{1,0:T(8,128)(2,1)} %bitcast.63), channel_id=1, source_target_pairs={{0,16},{2,18},{4,20},{6,22},{8,24},{10,26},{12,28},{14,30},{16,0},... | collective-permute-start | bytes 1179656 | tf_op jit(solution)/shard_map/ppermute | solution.py:570
  412.6 14.0 %collective-permute-start.12 = (bf16[1536,128]{1,0:T(8,128)(2,1)S(1)}, bf16[1536,128]{1,0:T(8,128)(2,1)S(1)}, u32[]{:S(2)}, u32[]{:S(2)}) collective-permute-start(bf16[1536,128]{1,0:T(8,128)(2,1)S(1)} %collective-permute-done.7.refs_1_), channel_id=1, source_target_pairs={{0,1},{1,0},{2,3},{3,2},{4,5},{5,4},{6,7},{7,6},{8,9},{9,8},{10,11... | collective-permute-start | bytes 1179656 | tf_op jit(solution)/shard_map/ppermute | solution.py:579
  413.9 15.0 %collective-permute-start.13 = (bf16[1536,128]{1,0:T(8,128)(2,1)S(1)}, bf16[1536,128]{1,0:T(8,128)(2,1)S(1)}, u32[]{:S(2)}, u32[]{:S(2)}) collective-permute-start(bf16[1536,128]{1,0:T(8,128)(2,1)S(1)} %collective-permute-done.6.refs_3_), channel_id=1, source_target_pairs={{0,1},{1,0},{2,3},{3,2},{4,5},{5,4},{6,7},{7,6},{8,9},{9,8},{10,11... | collective-permute-start | bytes 1179656 | tf_op jit(solution)/shard_map/ppermute | solution.py:579
  425.3 7.8 %collective-permute-start.11 = (bf16[1536,128]{1,0:T(8,128)(2,1)S(1)}, bf16[1536,128]{1,0:T(8,128)(2,1)S(1)}, u32[]{:S(2)}, u32[]{:S(2)}) collective-permute-start(bf16[1536,128]{1,0:T(8,128)(2,1)S(1)} %collective-permute-done.10.refs_2_), channel_id=1, source_target_pairs={{0,1},{1,0},{2,3},{3,2},{4,5},{5,4},{6,7},{7,6},{8,9},{9,8},{10,11... | collective-permute-start | bytes 1179656 | tf_op jit(solution)/shard_map/ppermute | solution.py:579
Sparse Core Ops, SparseCore 0:
  11.7 31.2 all-gather.8
  44.5 28.6 all-gather.10
  74.7 28.9 all-gather.12
  113.0 28.6 all-gather.14
